TPU v7x, 32 devices: a whole 2x2x4 slice. The times are simulated.
32 devices in a mesh: dp: 2 (over x), ep: 16 (over z, y, core).
Axes of the slice: x: 2, y: 2, z: 4, core: 2. Of those that a mesh axis runs over, the one named last changes fastest.
Arguments:
- hidden: bfloat16 [6, 1536, 1024], P('dp', 'ep'), may hold values from -6 to 6
- lengths: int32 [6], P('dp'), may hold values from 192 to 1536, as said below
- expert_ids: int32 [6, 1536, 8], P('dp', 'ep'), may hold values from 0 to 15, all different within a row
- pair_keep: int32 [6, 1536, 8], P('dp', 'ep'), may hold values 0 or 1
- attn_gain: bfloat16 [1024], P(('dp', 'ep')), may hold values from 0.25 to 1.75
- query_weight_matrix: bfloat16 [1024, 1024], P(('dp', 'ep')), may hold values from -0.1875 to 0.1875
- key_weight_matrix: bfloat16 [1024, 512], P(('dp', 'ep')), may hold values from -0.1875 to 0.1875
- value_weight_matrix: bfloat16 [1024, 512], P(('dp', 'ep')), may hold values from -0.1875 to 0.1875
- attention_output_weight: bfloat16 [1024, 1024], P(('dp', 'ep')), may hold values from -1.5 to 1.5
- moe_gain: bfloat16 [1024], P(('dp', 'ep')), may hold values from 0.25 to 1.75
- router_weight_matrix: bfloat16 [1024, 16], P(('dp', 'ep')), may hold values from -0.09375 to 0.09375
- w_gate_up: bfloat16 [16, 1024, 1024], P('ep'), may hold values from -0.1875 to 0.1875
- w_down: bfloat16 [16, 512, 1024], P('ep'), may hold values from -1 to 1
- out_grad: bfloat16 [6, 1536, 1024], P('dp', 'ep'), may hold values from -6 to 6
Outputs:
- output: bfloat16 [6, 1536, 1024], P('dp', 'ep')
- input_grad: float32 [6, 1536, 1024], P('dp', 'ep')
- attn_gain_grad: float32 [1024], P(('dp', 'ep'))
- w_query_grad: float32 [1024, 1024], P(('dp', 'ep'))
- w_key_grad: float32 [1024, 512], P(('dp', 'ep'))
- w_value_grad: float32 [1024, 512], P(('dp', 'ep'))
- w_out_grad: float32 [1024, 1024], P(('dp', 'ep'))
- moe_gain_grad: float32 [1024], P(('dp', 'ep'))
- w_router_grad: float32 [1024, 16], P(('dp', 'ep'))
- w_gate_up_grad: float32 [16, 1024, 1024], P('ep')
- w_down_grad: float32 [16, 512, 1024], P('ep')
Inputs may be any that keep to these rules, and one draw needn't show every extreme that they name: `lengths`: in every group of 3 consecutive sequences (one index of dp) one has length 1536. `expert_ids`: the 8 ids of a token are distinct.
All inputs are finite; a program needn't handle non-finite values. No bound on the sum of `pair_keep` on one device may be relied on, other than what follows from the above.
Results may differ from a plain program's by a relative error of at most 0.019.
Values may be sent and summed in bfloat16 or wider, within the bound.
No kernel may reach another device: no remote copies, remote signals or barrier semaphores. Data moves between devices by JAX's collectives and lax.ppermute only.
A program may use at most 256 MiB of HBM per device.

v0:
```python
import functools

import jax
import jax.numpy as jnp
from jax import lax
from jax.experimental import pallas as pl
from jax.experimental.pallas import tpu as pltpu
from jax.sharding import PartitionSpec as P

HD = 64
LANES = 128
SLAB = 256
WIDE = 512
PACK = 256
eps = 1e-05
theta_base = 10000.0
f32 = jnp.float32
bf16 = jnp.bfloat16
VMEM_LIMIT = 56 * 1024 * 1024


def dot(a, b):
    return lax.dot_general(a, b, (((1,), (0,)), ((), ())), preferred_element_type=f32)


def dot_nt(a, b):
    return lax.dot_general(a, b, (((1,), (1,)), ((), ())), preferred_element_type=f32)


def dot_tn(a, b):
    return lax.dot_general(a, b, (((0,), (0,)), ((), ())), preferred_element_type=f32)


def lanes_of(rows, width=LANES):
    return lax.broadcasted_iota(jnp.int32, (rows, width), 1)


def half_swap(x):
    lane = lanes_of(x.shape[0])
    return jnp.where(lane % HD < HD // 2, pltpu.roll(x, LANES - HD // 2, 1), pltpu.roll(x, HD // 2, 1))


def ep_shape(ep):
    zs = 4 if ep % 8 == 0 else 1
    return zs, ep // (2 * zs), 2


def fetch_from(ep, dz=0, dy=0, dc=0):
    zs, ys, cs = ep_shape(ep)
    pairs = []
    for z in range(zs):
        for y in range(ys):
            for c in range(cs):
                src = (((z + dz) % zs) * ys + (y + dy) % ys) * cs + (c + dc) % cs
                pairs.append((src, (z * ys + y) * cs + c))
    return pairs


def send_to(ep, **offset):
    return [(dst, src) for src, dst in fetch_from(ep, **offset)]


def phase(*values):
    return lax.optimization_barrier(values)


def phase_tree(*values):
    flat, tree = jax.tree.flatten(values)
    return jax.tree.unflatten(tree, phase(*flat))


def add_low(*parts):
    total = parts[0].astype(f32)
    for part in parts[1:]:
        total = total + part.astype(f32)
    return total.astype(bf16)


def project_kernel(place, carry, meta, *refs):
    blocks = refs[:place]
    w_ref, gain_ref, cos_ref, sin_ref = refs[place : place + 4]
    normed_ref, qkv_ref = refs[-2:]
    rows, _ = blocks[0].shape
    span = cos_ref.shape[0] // place
    seqs = rows // span
    lane = lanes_of(rows)
    for j in range(place):
        x = blocks[j][...].astype(f32)
        scale = lax.rsqrt(jnp.mean(x * x, axis=-1, keepdims=True) + eps)
        normed = (x * scale * gain_ref[...]).astype(bf16)
        normed_ref[0, j] = normed
        raw = dot(normed, w_ref[...])
        at = pl.ds(pl.multiple_of(meta[1 + j] * span, 32), span)
        cos = jnp.concatenate([cos_ref[at, :]] * seqs, axis=0)
        sin = jnp.concatenate([sin_ref[at, :]] * seqs, axis=0)
        both = raw[:, 0:LANES]
        both = (both * cos + half_swap(both) * sin).astype(bf16).astype(f32)
        both = jnp.where(lane < HD, both * HD ** (-0.5), both)
        qkv_ref[0, j, :, 0:LANES] = both.astype(bf16)
        qkv_ref[0, j, :, LANES:PACK] = jnp.where(lane < HD, raw[:, LANES:PACK], 0.0).astype(bf16)


def project(meta, blocks, w, gain, cos, sin, zs, dz, carried):
    rows, width = blocks[0].shape
    place = len(blocks)
    span = cos.shape[0] // (zs * place)

    def whole(a):
        return pl.BlockSpec(a.shape, lambda i, m: (0,) * a.ndim)

    table = pl.BlockSpec((place * span, LANES), lambda i, m: (lax.rem(m[0] + dz, zs), 0))
    args = list(blocks) + [w, gain, cos, sin]
    in_specs = [whole(a) for a in blocks] + [whole(w), whole(gain), table, table]
    aliases = {}
    if carried is not None:
        aliases = {1 + len(args): 0, 2 + len(args): 1}
        args += list(carried)
        in_specs += [pl.BlockSpec(memory_space=pl.ANY)] * 2
    return pl.pallas_call(
        functools.partial(project_kernel, place, carried is not None),
        grid_spec=pltpu.PrefetchScalarGridSpec(
            num_scalar_prefetch=1,
            grid=(1,),
            in_specs=in_specs,
            out_specs=(
                pl.BlockSpec((1, place, rows, width), lambda i, m: (dz, 0, 0, 0)),
                pl.BlockSpec((1, place, rows, PACK), lambda i, m: (dz, 0, 0, 0)),
            ),
        ),
        out_shape=(
            jax.ShapeDtypeStruct((zs, place, rows, width), bf16),
            jax.ShapeDtypeStruct((zs, place, rows, PACK), bf16),
        ),
        input_output_aliases=aliases,
        compiler_params=pltpu.CompilerParams(vmem_limit_bytes=VMEM_LIMIT),
        cost_estimate=pl.CostEstimate(
            flops=2 * place * rows * width * PACK,
            bytes_accessed=4 * place * rows * width,
            transcendentals=0,
        ),
        name="project_in",
    )(meta, *args)


def attend_kernel(
    replicas,
    meta,
    qkv_ref,
    out_ref,
    qk_ref,
    v_ref,
    qkt_ref,
    stat_ref,
    vt_ref,
    wide_ref,
):
    zs, place, rows, _ = qkv_ref.shape
    total = qk_ref.shape[1]
    span = total // (zs * place)
    s = pl.program_id(0)
    seqs = rows // span
    source = pl.ds(pl.multiple_of(s * span, 32), span)
    for d in range(zs):
        for j in range(place):
            at = pl.multiple_of((meta[seqs + 1 + d] * place + meta[seqs + 1 + zs + j]) * span, 32)
            qk_ref[0, pl.ds(at, span), :] = qkv_ref[d, j, source, 0:LANES]
            v_ref[0, pl.ds(at, span), :] = qkv_ref[d, j, source, LANES:PACK]
    for lo in range(0, total, SLAB):
        at = slice(lo, lo + SLAB)
        qkt_ref[0, :, at] = qk_ref[0, at, :].astype(f32).T.astype(bf16)
        vt_ref[:, at] = v_ref[0, at, :].astype(f32).T.astype(bf16)

    key_row = lax.broadcasted_iota(jnp.int32, (WIDE, WIDE), 0)
    query_col = lax.broadcasted_iota(jnp.int32, (WIDE, WIDE), 1)

    def one_slab(lo):
        hi = lo + WIDE
        qt = qkt_ref[0, 0:HD, lo:hi]
        diag = dot(qk_ref[0, lo:hi, HD:LANES], qt)
        diag = jnp.where(key_row <= query_col, diag, -jnp.inf)
        top = jnp.max(diag, axis=0, keepdims=True)
        if lo:
            full = dot(qk_ref[0, 0:lo, HD:LANES], qt)
            top = jnp.maximum(top, jnp.max(full, axis=0, keepdims=True))
        p_diag = jnp.exp(diag - top)
        row_total = jnp.sum(p_diag, axis=0, keepdims=True)
        out = dot(vt_ref[:, lo:hi], p_diag.astype(bf16))
        if lo:
            p_full = jnp.exp(full - top)
            row_total = row_total + jnp.sum(p_full, axis=0, keepdims=True)
            out = out + dot(vt_ref[:, 0:lo], p_full.astype(bf16))
        out = out[0:HD] / row_total
        stat_ref[0, 0:HD, lo:hi] = out
        stat_ref[0, HD : HD + 8, lo:hi] = jnp.broadcast_to(top + jnp.log(row_total), (8, WIDE))
        wide_ref[lo:hi, :] = jnp.concatenate([out, out], axis=0).T

    def no_slab(lo):
        stat_ref[0, :, lo : lo + WIDE] = jnp.zeros((HD + 8, WIDE), f32)
        wide_ref[lo : lo + WIDE, :] = jnp.zeros((WIDE, LANES), f32)

    for i, lo in enumerate(range(0, total, WIDE)):
        if replicas > 1:
            mine = meta[seqs] == i % replicas
            pl.when(mine)(functools.partial(one_slab, lo))
            pl.when(jnp.logical_not(mine))(functools.partial(no_slab, lo))
        else:
            one_slab(lo)

    half = span // 2
    for e in range(total // span):
        upper = wide_ref[e * span : e * span + half, :]
        lower = wide_ref[e * span + half : (e + 1) * span, :]
        out_ref[e] = jnp.where(lanes_of(half) < HD, upper, lower).astype(bf16)


def attend(meta, qkv, seqs, replicas):
    zs, place, rows, _ = qkv.shape
    span = rows // seqs
    total = zs * place * span
    return pl.pallas_call(
        functools.partial(attend_kernel, replicas),
        grid=(seqs,),
        out_shape=(
            jax.ShapeDtypeStruct((total // span, seqs * (span // 2), LANES), bf16),
            jax.ShapeDtypeStruct((seqs, total, LANES), bf16),
            jax.ShapeDtypeStruct((seqs, total, LANES), bf16),
            jax.ShapeDtypeStruct((seqs, LANES, total), bf16),
            jax.ShapeDtypeStruct((seqs, HD + 8, total), f32),
        ),
        in_specs=[
            pl.BlockSpec(memory_space=pltpu.SMEM),
            pl.BlockSpec(qkv.shape, lambda s: (0, 0, 0, 0)),
        ],
        out_specs=(
            pl.BlockSpec((total // span, span // 2, LANES), lambda s: (0, s, 0)),
            pl.BlockSpec((1, total, LANES), lambda s: (s, 0, 0)),
            pl.BlockSpec((1, total, LANES), lambda s: (s, 0, 0)),
            pl.BlockSpec((1, LANES, total), lambda s: (s, 0, 0)),
            pl.BlockSpec((1, HD + 8, total), lambda s: (s, 0, 0)),
        ),
        scratch_shapes=[pltpu.VMEM((LANES, total), bf16), pltpu.VMEM((total, LANES), f32)],
        compiler_params=pltpu.CompilerParams(vmem_limit_bytes=VMEM_LIMIT),
        cost_estimate=pl.CostEstimate(
            flops=4 * seqs * total * total * LANES,
            bytes_accessed=4 * seqs * total * PACK,
            transcendentals=seqs * total * total // 2,
        ),
        name="attend_forward",
    )(meta, qkv)


def gates_of(normed, wr_ref, code):
    logits = jnp.where(code != 0, dot(normed, wr_ref[...]), -1e30)
    powers = jnp.exp(logits - jnp.max(logits, axis=-1, keepdims=True))
    return powers / jnp.sum(powers, axis=-1, keepdims=True)


def middle_kernel(
    seqs,
    recv_ref,
    hid_ref,
    wo_ref,
    gain_ref,
    wr_ref,
    code_ref,
    res_ref,
    pay_ref,
    mixed_ref,
    gate_ref,
):
    heads, half_rows, _ = recv_ref.shape
    width = hid_ref.shape[1]
    half = half_rows // seqs
    low = lanes_of(half_rows) < HD
    uppers, lowers = [], []
    for j in range(heads // 2):
        a = recv_ref[2 * j].astype(f32)
        b = recv_ref[2 * j + 1].astype(f32)
        uppers.append(jnp.where(low, a, pltpu.roll(b, HD, 1)).astype(bf16))
        lowers.append(jnp.where(low, pltpu.roll(a, HD, 1), b).astype(bf16))
    upper = jnp.concatenate(uppers, axis=1)
    lower = jnp.concatenate(lowers, axis=1)
    pieces = []
    for s in range(seqs):
        pieces += [upper[s * half : (s + 1) * half], lower[s * half : (s + 1) * half]]
    mixed = jnp.concatenate(pieces, axis=0)
    mixed_ref[...] = mixed
    res = hid_ref[...].astype(f32) + dot(mixed, wo_ref[...])
    res_ref[...] = res
    scale = lax.rsqrt(jnp.mean(res * res, axis=-1, keepdims=True) + eps)
    normed = (res * scale * gain_ref[...]).astype(bf16)
    gate_ref[...] = gates_of(normed, wr_ref, code_ref[...])
    pay_ref[...] = normed


def middle(seqs, recv, hid, wo, gain, wr, code):
    rows, width = hid.shape
    vmem = pl.BlockSpec(memory_space=pltpu.VMEM)
    return pl.pallas_call(
        functools.partial(middle_kernel, seqs),
        out_shape=(
            jax.ShapeDtypeStruct((rows, width), f32),
            jax.ShapeDtypeStruct((rows, width), bf16),
            jax.ShapeDtypeStruct((rows, width), bf16),
            jax.ShapeDtypeStruct((rows, LANES), f32),
        ),
        in_specs=[vmem] * 6,
        out_specs=(vmem,) * 4,
        compiler_params=pltpu.CompilerParams(vmem_limit_bytes=VMEM_LIMIT),
        cost_estimate=pl.CostEstimate(
            flops=4 * rows * width * width, bytes_accessed=4 * width * width, transcendentals=0
        ),
        name="project_out",
    )(recv, hid, wo, gain, wr, code)


def expert_kernel(place, cap, zs, dz, first, meta, *refs):
    pay_in = refs[0:place]
    up_in, wgu_in, wd_in, wr_ref = refs[place : place + 4]
    rest = refs[place + 4 + (0 if first else 6) :]
    near_out, far_out, mnear_out, mfar_out, x_out, pg_out, act_out, both_out = rest[:8]
    pay, up, code, wgu, wd, back_s, moe_s, x_s, pg_s, act_s, both_s, in_sem, out_sem = rest[8:]
    rows, width = pay_in[0].shape
    units = wd.shape[0]
    halves = place // 2
    expert = meta[0]
    plane = lax.rem(meta[1] + dz, zs)
    loads = {}
    order = []
    for j in range(place):
        loads["p", j] = pltpu.make_async_copy(pay_in[j], pay.at[j], in_sem.at[2 * j])
        source = up_in.at[plane * place + meta[2 + j]]
        loads["u", j] = pltpu.make_async_copy(
            source.at[pl.ds(0, rows)], up.at[j], in_sem.at[2 * j + 1]
        )
        loads["c", j] = pltpu.make_async_copy(
            source.at[pl.ds(rows, code.shape[1]), pl.ds(0, code.shape[2])],
            code.at[j],
            in_sem.at[2 * place + 2 + j],
        )
    loads["gu"] = pltpu.make_async_copy(wgu_in, wgu, in_sem.at[2 * place])
    loads["d"] = pltpu.make_async_copy(wd_in, wd, in_sem.at[2 * place + 1])
    order = [("c", j) for j in range(place)]
    order += [("p", j) for j in range(halves)] + ["gu", "d"]
    order += [("u", j) for j in range(halves)]
    order += [("p", j) for j in range(halves, place)] + [("u", j) for j in range(halves, place)]
    for key in order:
        loads[key].start()
    stores = []

    def store(src, dst):
        copy = pltpu.make_async_copy(src, dst, out_sem.at[len(stores)])
        copy.start()
        stores.append(copy)

    def save(h, value, buf, out):
        own = pl.ds(h * halves * cap, halves * cap)
        buf[own, :] = value
        store(buf.at[own], out.at[dz, own])

    lane = lanes_of(rows)
    slot_row = lax.broadcasted_iota(jnp.int32, (cap, rows), 0)
    slot_col = lax.broadcasted_iota(jnp.int32, (rows, cap), 1)
    code_row = lax.broadcasted_iota(jnp.int32, (code.shape[1], rows), 0)
    cap_lane = lanes_of(cap)
    line_row = lax.broadcasted_iota(jnp.int32, code.shape[1:], 0)
    slot_wide = lax.broadcasted_iota(jnp.int32, (cap, code.shape[2]), 0)
    for h in range(2):
        mine = range(h * halves, (h + 1) * halves)
        for j in mine:
            loads["c", j].wait()
            loads["p", j].wait()
        outs_of, xs, gates = [], [], []
        into, into_wide = [], []
        for j in mine:
            lines = code[j].astype(f32)
            blank = jnp.zeros((LANES - lines.shape[0], lines.shape[1]), f32)
            codes = jnp.concatenate([lines, blank], axis=0).T[0:rows]
            column = jnp.sum(jnp.where(lane == expert, codes, 0.0), axis=1, keepdims=True)
            line = jnp.sum(
                jnp.where(code_row == expert, lines[:, 0:rows], 0.0), axis=0, keepdims=True
            )
            into.append(jnp.where(line.astype(jnp.int32) == slot_row + 1, 1.0, 0.0).astype(bf16))
            line = jnp.sum(jnp.where(line_row == expert, lines, 0.0), axis=0, keepdims=True)
            into_wide.append(
                jnp.where(line.astype(jnp.int32) == slot_wide + 1, 1.0, 0.0).astype(bf16)
            )
            outs_of.append(
                jnp.where(column.astype(jnp.int32) == slot_col + 1, 1.0, 0.0).astype(bf16)
            )
            xs.append(dot(into[-1], pay[j]).astype(bf16))
            gate = gates_of(xs[-1], wr_ref, dot(into[-1], codes.astype(bf16)))
            gates.append(jnp.sum(jnp.where(cap_lane == expert, gate, 0.0), axis=1, keepdims=True))
        x = jnp.concatenate(xs, axis=0)
        gate_prob = jnp.concatenate(gates, axis=0)
        if h == 0:
            loads["gu"].wait()
        save(h, x, x_s, x_out)
        gate_up = dot(x, wgu[...])
        gate = gate_up[:, 0:units]
        high = gate_up[:, units:]
        sig = jax.nn.sigmoid(gate)
        silu = gate * sig
        act = (silu * high).astype(bf16)
        if h == 0:
            loads["d"].wait()
        save(h, act, act_s, act_out)
        made = dot(act, wd[...]).astype(bf16).astype(f32)
        for j in mine:
            loads["u", j].wait()
        upstream = jnp.concatenate([dot(into[k], up[j]) for k, j in enumerate(mine)], axis=0)
        gate_grad = jnp.sum(made * upstream, axis=-1, keepdims=True)
        moe = (made * gate_prob).astype(bf16)
        pair_grad = (upstream * gate_prob).astype(bf16)
        for k, j in enumerate(mine):
            part = slice(k * cap, (k + 1) * cap)
            moe_s[j] = dot(outs_of[k], moe[part]).astype(bf16)
        store(moe_s.at[pl.ds(h * halves, halves)], (mnear_out if h == 0 else mfar_out).at[dz])
        save(h, pair_grad, pg_s, pg_out)
        act_grad = dot_nt(pair_grad, wd[...])
        both = jnp.concatenate(
            [act_grad * high * (sig * (1.0 + gate * (1.0 - sig))), act_grad * silu], axis=1
        ).astype(bf16)
        save(h, both, both_s, both_out)
        back = dot_nt(both, wgu[...]).astype(bf16)
        upper = gate_grad.astype(bf16).astype(f32)
        pair_lane = lanes_of(halves * cap)
        pair = jnp.where(pair_lane == 0, upper, gate_grad - upper)
        for k, j in enumerate(mine):
            part = slice(k * cap, (k + 1) * cap)
            back_s[j, 0:rows, :] = dot(outs_of[k], back[part]).astype(bf16)
            found = dot(pair[part].T[0:16].astype(bf16), into_wide[k])
            back_s[j, rows:, :] = jnp.zeros((code.shape[1], width), bf16)
            for row, at in ((0, 0), (1, width // 2)):
                value = jnp.where(line_row == expert, found[row : row + 1], 0.0)
                back_s[j, rows:, at : at + code.shape[2]] = value.astype(bf16)
        store(back_s.at[pl.ds(h * halves, halves)], near_out if h == 0 else far_out)
    for copy in stores:
        copy.wait()


def experts(meta, pays, upstream, wgu, wd, wr, cap, zs, dz, carried):
    place = len(pays)
    rows, width = pays[0].shape
    units = wd.shape[0]
    first = carried is None
    anyspace = pl.BlockSpec(memory_space=pl.ANY)
    args = list(pays) + [upstream, wgu, wd, wr]
    code_rows = upstream.shape[1] - rows
    aliases = {}
    if not first:
        aliases = {1 + len(args) + k: 2 + k for k in range(6)}
        args += list(carried)
    half = jax.ShapeDtypeStruct((place // 2, rows + code_rows, width), bf16)
    slots = place * cap
    return pl.pallas_call(
        functools.partial(expert_kernel, place, cap, zs, dz, first),
        out_shape=(
            half,
            half,
            jax.ShapeDtypeStruct((zs, place // 2, rows, width), bf16),
            jax.ShapeDtypeStruct((zs, place // 2, rows, width), bf16),
            jax.ShapeDtypeStruct((zs, slots, width), bf16),
            jax.ShapeDtypeStruct((zs, slots, width), bf16),
            jax.ShapeDtypeStruct((zs, slots, units), bf16),
            jax.ShapeDtypeStruct((zs, slots, 2 * units), bf16),
        ),
        in_specs=[pl.BlockSpec(memory_space=pltpu.SMEM)]
        + [anyspace] * (place + 3)
        + [pl.BlockSpec(memory_space=pltpu.VMEM)]
        + [anyspace] * (len(args) - place - 4),
        out_specs=(anyspace,) * 8,
        scratch_shapes=[
            pltpu.VMEM((place, rows, width), bf16),
            pltpu.VMEM((place, rows, width), bf16),
            pltpu.VMEM((place, code_rows, -(-rows // LANES) * LANES), bf16),
            pltpu.VMEM(wgu.shape, bf16),
            pltpu.VMEM(wd.shape, bf16),
            pltpu.VMEM((place, rows + code_rows, width), bf16),
            pltpu.VMEM((place, rows, width), bf16),
            pltpu.VMEM((slots, width), bf16),
            pltpu.VMEM((slots, width), bf16),
            pltpu.VMEM((slots, units), bf16),
            pltpu.VMEM((slots, 2 * units), bf16),
            pltpu.SemaphoreType.DMA((3 * place + 2,)),
            pltpu.SemaphoreType.DMA((12,)),
        ],
        input_output_aliases=aliases,
        compiler_params=pltpu.CompilerParams(vmem_limit_bytes=VMEM_LIMIT),
        cost_estimate=pl.CostEstimate(
            flops=16 * slots * width * units, bytes_accessed=12 * slots * width, transcendentals=0
        ),
        name="experts",
    )(meta, *args)


def turn_kernel(nparts, seqs, meta, *refs):
    parts = refs[:nparts]
    (
        res_ref,
        up_ref,
        gate_ref,
        code_ref,
        wr_ref,
        gain_ref,
        wo_ref,
        resgrad_ref,
        branch_ref,
        out_ref,
        logit_ref,
        gaingrad_ref,
    ) = refs[nparts:]
    rows, width = res_ref.shape
    span = rows // seqs
    total = parts[0][...].astype(f32)
    for part in parts[1:]:
        total = total + part[...].astype(f32)
    held = -(-rows // LANES) * LANES
    lines = total[rows:, 0:held] + total[rows:, width // 2 : width // 2 + held]
    blank = jnp.zeros((LANES - lines.shape[0], held), f32)
    gate_grad = jnp.concatenate([lines, blank], axis=0).T[0:rows]
    gate_grad = jnp.where(code_ref[...] > 0, gate_grad, 0.0)
    gates = gate_ref[...]
    logit_grad = gates * (gate_grad - jnp.sum(gates * gate_grad, axis=-1, keepdims=True))
    logit_ref[...] = logit_grad
    normed_grad = total[0:rows] + lax.dot_general(
        logit_grad,
        wr_ref[...].astype(f32),
        (((1,), (1,)), ((), ())),
        preferred_element_type=f32,
        precision=lax.Precision.HIGHEST,
    )
    res = res_ref[...]
    scale = lax.rsqrt(jnp.mean(res * res, axis=-1, keepdims=True) + eps)
    gaingrad_ref[...] = jnp.sum(normed_grad * (res * scale), axis=0, keepdims=True)
    scaled = normed_grad * gain_ref[...]
    row = meta[seqs] + lax.broadcasted_iota(jnp.int32, (span, 1), 0)
    valid = jnp.concatenate([(row < meta[s]).astype(f32) for s in range(seqs)], axis=0)
    upstream = jnp.where(valid > 0, up_ref[...].astype(f32), 0.0)
    centre = jnp.mean(scaled * res, axis=-1, keepdims=True)
    res_grad = upstream + scaled * scale - res * (scale * scale * scale * centre)
    resgrad_ref[...] = res_grad
    branch = res_grad.astype(bf16)
    branch_ref[...] = branch
    mixed = dot_nt(branch, wo_ref[...]).astype(bf16).astype(f32)
    half = span // 2
    low = lanes_of(half) < HD
    for s in range(seqs):
        at = slice(s * half, (s + 1) * half)
        for j in range(out_ref.shape[0] // 2):
            cols = slice(j * LANES, (j + 1) * LANES)
            upper = mixed[s * span : s * span + half, cols]
            lower = mixed[s * span + half : (s + 1) * span, cols]
            out_ref[2 * j, at] = jnp.where(low, upper, pltpu.roll(lower, HD, 1)).astype(bf16)
            out_ref[2 * j + 1, at] = jnp.where(low, pltpu.roll(upper, HD, 1), lower).astype(bf16)


def turn(meta, seqs, parts, res, up, gates, code, wr, gain, wo):
    rows, width = res.shape
    heads = wo.shape[0] // HD
    vmem = pl.BlockSpec(memory_space=pltpu.VMEM)
    return pl.pallas_call(
        functools.partial(turn_kernel, len(parts), seqs),
        out_shape=(
            jax.ShapeDtypeStruct((rows, width), f32),
            jax.ShapeDtypeStruct((rows, width), bf16),
            jax.ShapeDtypeStruct((heads, rows // 2, LANES), bf16),
            jax.ShapeDtypeStruct((rows, LANES), f32),
            jax.ShapeDtypeStruct((1, width), f32),
        ),
        in_specs=[pl.BlockSpec(memory_space=pltpu.SMEM)] + [vmem] * (len(parts) + 7),
        out_specs=(vmem,) * 5,
        compiler_params=pltpu.CompilerParams(vmem_limit_bytes=VMEM_LIMIT),
        cost_estimate=pl.CostEstimate(
            flops=4 * rows * width * width, bytes_accessed=4 * width * width, transcendentals=0
        ),
        name="turn_back",
    )(meta, *parts, res, up, gates, code, wr, gain, wo)


def back_kernel(
    replicas,
    meta,
    grad_ref,
    qk_ref,
    v_ref,
    qkt_ref,
    stat_ref,
    cos_ref,
    sin_ref,
    out_ref,
    do_ref,
    dk_ref,
    dv_ref,
    dqt_ref,
):
    zs, place, rows, _ = out_ref.shape
    total = qk_ref.shape[1]
    span = total // (zs * place)
    seqs = rows // span
    s = pl.program_id(0)
    half = span // 2
    for e in range(total // span):
        chunk = grad_ref[e].astype(f32)
        do_ref[e * span : e * span + half, :] = chunk
        do_ref[e * span + half : (e + 1) * span, :] = pltpu.roll(chunk, HD, 1)
    dk_ref[...] = jnp.zeros_like(dk_ref)
    dv_ref[...] = jnp.zeros_like(dv_ref)
    key_row = lax.broadcasted_iota(jnp.int32, (SLAB, SLAB), 0)
    query_col = lax.broadcasted_iota(jnp.int32, (SLAB, SLAB), 1)
    def one_slab(lo):
        hi = lo + 2 * SLAB
        mid = lo + SLAB
        grad = do_ref[lo:hi, :]
        grad_low = grad.astype(bf16)
        grad_t = grad.T[0:HD]
        delta = jnp.sum(grad_t * stat_ref[0, 0:HD, lo:hi], axis=0, keepdims=True)
        grad_t = grad_t.astype(bf16)
        log_total = stat_ref[0, HD : HD + 1, lo:hi]

        def piece(start, stop, first, last, masked):
            cols = slice(first - lo, last - lo)
            scores = dot(qk_ref[0, start:stop, HD:LANES], qkt_ref[0, 0:HD, first:last])
            probs = jnp.exp(scores - log_total[:, cols])
            if masked:
                probs = jnp.where(key_row <= query_col, probs, 0.0)
            prob_grad = dot(v_ref[0, start:stop, 0:HD], grad_t[:, cols])
            score_grad = (probs * (prob_grad - delta[:, cols])).astype(bf16)
            dv_ref[start:stop, :] += dot(probs.astype(bf16), grad_low[cols])
            dk_ref[start:stop, :] += dot(score_grad, qk_ref[0, first:last, :])
            return dot(qkt_ref[0, :, start:stop], score_grad)

        moved = piece(lo, mid, lo, mid, True)
        moved_next = piece(mid, hi, mid, hi, True) + piece(lo, mid, mid, hi, False)
        if lo:
            full = piece(0, lo, lo, hi, False)
            moved = moved + full[:, 0:SLAB]
            moved_next = moved_next + full[:, SLAB:]
        dqt_ref[:, lo:mid] = moved
        dqt_ref[:, mid:hi] = moved_next

    def no_slab(lo):
        dqt_ref[:, lo : lo + 2 * SLAB] = jnp.zeros((LANES, 2 * SLAB), f32)

    for i, lo in enumerate(range(0, total, 2 * SLAB)):
        if replicas > 1:
            mine = meta[seqs] == i % replicas
            pl.when(mine)(functools.partial(one_slab, lo))
            pl.when(jnp.logical_not(mine))(functools.partial(no_slab, lo))
        else:
            one_slab(lo)

    low = lanes_of(SLAB) < HD
    for lo in range(0, total, SLAB):
        at = slice(lo, lo + SLAB)
        both = jnp.where(low, dk_ref[at, :], dqt_ref[:, at].T * HD ** (-0.5))
        both = pltpu.roll(both, HD, 1)
        dk_ref[at, :] = both * cos_ref[at, :] - half_swap(both) * sin_ref[at, :]
        dv_ref[at, :] = jnp.where(low, dv_ref[at, :], 0.0)
    dest = pl.ds(pl.multiple_of(s * span, 32), span)
    for d in range(zs):
        for j in range(place):
            at = pl.multiple_of((meta[seqs + 1 + d] * place + meta[seqs + 1 + zs + j]) * span, 32)
            out_ref[d, j, dest, 0:LANES] = dk_ref[pl.ds(at, span), :].astype(bf16)
            out_ref[d, j, dest, LANES:PACK] = dv_ref[pl.ds(at, span), :].astype(bf16)


def back(meta, grads, qk, v, qkt, stat, cos, sin, shape, seqs, replicas):
    total = qk.shape[1]
    span = total // grads.shape[0]
    return pl.pallas_call(
        functools.partial(back_kernel, replicas),
        grid=(seqs,),
        out_shape=jax.ShapeDtypeStruct(shape, bf16),
        in_specs=[
            pl.BlockSpec(memory_space=pltpu.SMEM),
            pl.BlockSpec((total // span, span // 2, LANES), lambda s: (0, s, 0)),
            pl.BlockSpec((1, total, LANES), lambda s: (s, 0, 0)),
            pl.BlockSpec((1, total, LANES), lambda s: (s, 0, 0)),
            pl.BlockSpec((1, LANES, total), lambda s: (s, 0, 0)),
            pl.BlockSpec((1, HD + 8, total), lambda s: (s, 0, 0)),
            pl.BlockSpec((total, LANES), lambda s: (0, 0)),
            pl.BlockSpec((total, LANES), lambda s: (0, 0)),
        ],
        out_specs=pl.BlockSpec(shape, lambda s: (0, 0, 0, 0)),
        scratch_shapes=[
            pltpu.VMEM((total, LANES), f32),
            pltpu.VMEM((total, LANES), f32),
            pltpu.VMEM((total, LANES), f32),
            pltpu.VMEM((LANES, total), f32),
        ],
        compiler_params=pltpu.CompilerParams(vmem_limit_bytes=VMEM_LIMIT),
        cost_estimate=pl.CostEstimate(
            flops=10 * seqs * total * total * LANES,
            bytes_accessed=6 * seqs * total * PACK,
            transcendentals=seqs * total * total // 2,
        ),
        name="attend_backward",
    )(meta, grads, qk, v, qkt, stat, cos, sin)


def expert_grads_kernel(x_ref, both_ref, act_ref, pg_ref, *refs):
    outs, acc_ref = refs[:-1], refs[-1]
    width = x_ref.shape[2]

    @pl.when(pl.program_id(0) == 0)
    def _():
        acc_ref[...] = jnp.zeros_like(acc_ref)

    acc_ref[0:width, :] += dot_tn(x_ref[0], both_ref[0])
    acc_ref[width:, :] += dot_tn(act_ref[0], pg_ref[0])

    @pl.when(pl.program_id(0) == pl.num_programs(0) - 1)
    def _():
        for k, out_ref in enumerate(outs):
            rows = out_ref.shape[0]
            out_ref[...] = acc_ref[k * rows : (k + 1) * rows, :].astype(bf16)


def expert_grads(x, both, act, pg):
    zs, slots, width = x.shape
    units = act.shape[2]
    pieces = 4
    piece = (width + units) // pieces

    def block(a):
        return pl.BlockSpec((1,) + a.shape[1:], lambda i: (i, 0, 0))

    return pl.pallas_call(
        expert_grads_kernel,
        grid=(zs,),
        out_shape=(jax.ShapeDtypeStruct((piece, width), bf16),) * pieces,
        in_specs=[block(a) for a in (x, both, act, pg)],
        out_specs=(pl.BlockSpec((piece, width), lambda i: (0, 0)),) * pieces,
        scratch_shapes=[pltpu.VMEM((width + units, width), f32)],
        compiler_params=pltpu.CompilerParams(vmem_limit_bytes=VMEM_LIMIT),
        cost_estimate=pl.CostEstimate(
            flops=6 * zs * slots * width * units, bytes_accessed=8 * zs * slots * width, transcendentals=0
        ),
        name="expert_grads",
    )(x, both, act, pg)


def late_kernel(column, mixed_ref, branch_ref, pay_ref, logit_ref, gain_ref, out_ref):
    width = mixed_ref.shape[1]
    out_ref[:, 0:width] = dot_tn(mixed_ref[...], branch_ref[...]).astype(bf16)
    logit = logit_ref[...]
    high = logit.astype(bf16)
    low = (logit - high.astype(f32)).astype(bf16)
    normed = pay_ref[...]
    side = dot_tn(normed, high) + dot_tn(normed, low)
    gain = jnp.broadcast_to(gain_ref[...], (LANES, width)).T
    out_ref[:, width:] = jnp.where(lanes_of(width) == column, gain, side).astype(bf16)


def late_grads(column, mixed, branch, pay, logit, gain):
    rows, width = mixed.shape
    vmem = pl.BlockSpec(memory_space=pltpu.VMEM)
    return pl.pallas_call(
        functools.partial(late_kernel, column),
        out_shape=jax.ShapeDtypeStruct((width, width + LANES), bf16),
        in_specs=[vmem] * 5,
        out_specs=vmem,
        compiler_params=pltpu.CompilerParams(vmem_limit_bytes=VMEM_LIMIT),
        cost_estimate=pl.CostEstimate(
            flops=2 * rows * width * width, bytes_accessed=4 * width * width, transcendentals=0
        ),
        name="late_grads",
    )(mixed, branch, pay, logit, gain)


def head_grads_kernel(dqkv_ref, normed_ref, out_ref, acc_ref):
    _, place, rows, pack = dqkv_ref.shape

    @pl.when(pl.program_id(0) == 0)
    def _():
        acc_ref[...] = jnp.zeros_like(acc_ref)

    left = dqkv_ref[0].reshape(place * rows, pack)
    acc_ref[...] += dot_tn(left, normed_ref[0].reshape(place * rows, normed_ref.shape[3]))

    @pl.when(pl.program_id(0) == pl.num_programs(0) - 1)
    def _():
        out_ref[...] = acc_ref[...].T.astype(bf16)


def head_grads(dqkv, normed):
    zs, place, rows, width = normed.shape
    return pl.pallas_call(
        head_grads_kernel,
        grid=(zs,),
        out_shape=jax.ShapeDtypeStruct((width, PACK), bf16),
        in_specs=[
            pl.BlockSpec((1, place, rows, PACK), lambda i: (i, 0, 0, 0)),
            pl.BlockSpec((1, place, rows, width), lambda i: (i, 0, 0, 0)),
        ],
        out_specs=pl.BlockSpec((width, PACK), lambda i: (0, 0)),
        scratch_shapes=[pltpu.VMEM((PACK, width), f32)],
        compiler_params=pltpu.CompilerParams(vmem_limit_bytes=VMEM_LIMIT),
        cost_estimate=pl.CostEstimate(
            flops=2 * zs * place * rows * width * PACK,
            bytes_accessed=2 * zs * place * rows * width,
            transcendentals=0,
        ),
        name="head_grads",
    )(dqkv, normed)


def spread_kernel(dqkv_ref, w_ref, near_ref, far_ref):
    _, place, rows, pack = dqkv_ref.shape
    for ref, first in ((near_ref, 0), (far_ref, place // 2)):
        for j in range(place // 2):
            ref[0, j] = dot_nt(dqkv_ref[0, first + j], w_ref[...]).astype(bf16)


def spread(dqkv, w, picked):
    _, place, rows, pack = dqkv.shape
    width = w.shape[0]
    first, step = picked[0], (picked[1] - picked[0] if len(picked) > 1 else 0)
    half = jax.ShapeDtypeStruct((len(picked), place // 2, rows, width), bf16)
    out = pl.BlockSpec((1, place // 2, rows, width), lambda i: (i, 0, 0, 0))
    return pl.pallas_call(
        spread_kernel,
        grid=(len(picked),),
        out_shape=(half, half),
        in_specs=[
            pl.BlockSpec((1, place, rows, pack), lambda i: (first + i * step, 0, 0, 0)),
            pl.BlockSpec(w.shape, lambda i: (0, 0)),
        ],
        out_specs=(out, out),
        compiler_params=pltpu.CompilerParams(vmem_limit_bytes=VMEM_LIMIT),
        cost_estimate=pl.CostEstimate(
            flops=2 * len(picked) * place * rows * pack * width,
            bytes_accessed=2 * len(picked) * place * rows * width,
            transcendentals=0,
        ),
        name="spread",
    )(dqkv, w)


def finish_kernel(nparts, *refs):
    hid_ref, gain_ref, resgrad_ref = refs[0:3]
    parts = refs[3 : 3 + nparts]
    out_ref = refs[-1]
    total = parts[0][...].astype(f32)
    for part in parts[1:]:
        total = total + part[...].astype(f32)
    x = hid_ref[...].astype(f32)
    scale = lax.rsqrt(jnp.mean(x * x, axis=-1, keepdims=True) + eps)
    scaled = total * gain_ref[...]
    centre = jnp.mean(scaled * x, axis=-1, keepdims=True)
    out_ref[...] = resgrad_ref[...] + scaled * scale - x * (scale * scale * scale * centre)


def finish(hidden, gain, resgrad, parts):
    vmem = pl.BlockSpec(memory_space=pltpu.VMEM)
    return pl.pallas_call(
        functools.partial(finish_kernel, len(parts)),
        out_shape=jax.ShapeDtypeStruct(hidden.shape, f32),
        in_specs=[vmem] * (3 + len(parts)),
        out_specs=vmem,
        compiler_params=pltpu.CompilerParams(vmem_limit_bytes=VMEM_LIMIT),
        name="input_grad",
    )(hidden, gain, resgrad, *parts)


def body(
    hidden,
    lengths,
    expert_ids,
    pair_keep,
    attn_gain,
    query_weight_matrix,
    key_weight_matrix,
    value_weight_matrix,
    attention_output_weight,
    moe_gain,
    router_weight_matrix,
    w_gate_up,
    w_down,
    out_grad,
):
    seqs, span, width = hidden.shape
    rows = seqs * span
    top_k = expert_ids.shape[2]
    ep = lax.axis_size("ep")
    dp = lax.axis_size("dp")
    zs, ys, _ = ep_shape(ep)
    place = 2 * ys
    me = lax.axis_index("ep").astype(jnp.int32)
    expert_count = w_gate_up.shape[0] * ep
    capacity = max(2, rows * top_k // expert_count)
    cap = -(-capacity // 16) * 16
    heads = query_weight_matrix.shape[1] // HD
    kv_heads = key_weight_matrix.shape[1] // HD
    replicas = ep // heads
    total = span * ep
    own_rows = query_weight_matrix.shape[0]
    hidden = hidden.reshape(rows, width)
    out_grad = out_grad.reshape(rows, width)

    def per_head(weight, count):
        split = weight.reshape(own_rows, count, HD).transpose(1, 0, 2)
        return jnp.repeat(split, heads // count, axis=0)

    small = jnp.concatenate(
        [router_weight_matrix, attn_gain[:, None], moe_gain[:, None]], axis=1
    )
    small = jnp.pad(small, ((0, 0), (0, PACK - 3 * HD - small.shape[1])))
    packed = jnp.concatenate(
        [
            per_head(query_weight_matrix, heads),
            per_head(key_weight_matrix, kv_heads),
            per_head(value_weight_matrix, kv_heads),
            jnp.broadcast_to(small[None], (heads,) + small.shape),
        ],
        axis=2,
    )
    packed = jnp.repeat(packed, replicas, axis=0)
    packed = jnp.broadcast_to(packed[None], (dp,) + packed.shape).reshape(
        dp * ep, own_rows, PACK
    )
    packed = lax.all_to_all(packed, ("dp", "ep"), split_axis=0, concat_axis=0, tiled=True)
    head_w = packed.reshape(dp * ep * own_rows, PACK)
    at = 3 * HD
    wr = jnp.pad(head_w[:, at : at + expert_count], ((0, 0), (0, LANES - expert_count)))
    gains = head_w[:, at + expert_count : at + expert_count + 2].astype(f32)
    gain_one = gains[:, 0].reshape(1, width)
    gain_two = gains[:, 1].reshape(1, width)
    head_w = jnp.where(jnp.arange(PACK)[None, :] < at, head_w, jnp.zeros((), bf16))

    positions = me * span + jnp.arange(span, dtype=jnp.int32)
    is_valid = positions[None, :] < lengths[:, None]
    expert_range = jnp.arange(LANES, dtype=jnp.int32)
    hit = expert_ids[..., None] == expert_range
    chosen = jnp.any(hit, axis=2).reshape(rows, LANES).astype(f32)
    live = jnp.any(hit & (pair_keep[..., None] > 0), axis=2) & is_valid[..., None]
    live = live.reshape(rows, LANES).astype(bf16)
    earlier = jnp.arange(rows)[:, None] > jnp.arange(rows)[None, :]
    slot = jnp.dot(earlier.astype(bf16), live, preferred_element_type=f32)
    code = jnp.where((slot < capacity) & (live > 0), slot + 1.0, -chosen)
    code_rows = -(-expert_count // 16) * 16
    lines = jnp.pad(code[:, 0:code_rows].T.astype(bf16), ((0, 0), (0, width - rows)))
    lifted = jnp.concatenate([out_grad, lines])

    rates = theta_base ** (-2.0 * jnp.arange(HD // 2, dtype=f32) / HD)
    angle = jnp.arange(total, dtype=jnp.int32).astype(f32)[:, None] * rates[None, :]
    cos = jnp.tile(jnp.cos(angle), (1, 4))
    sin = jnp.sin(angle)
    sin = jnp.concatenate([-sin, sin, -sin, sin], axis=1)
    core = me % 2
    col = (me // 2) % ys
    plane = me // place
    planes = (plane + jnp.arange(zs, dtype=jnp.int32)) % zs
    rows_at = (col + jnp.arange(ys, dtype=jnp.int32)) % ys
    places = jnp.concatenate([rows_at * 2 + core, rows_at * 2 + 1 - core])
    replica = me % replicas if replicas > 1 else jnp.zeros((), jnp.int32)
    attend_meta = jnp.concatenate([lengths, replica[None], planes, places]).astype(jnp.int32)
    expert_meta = jnp.concatenate([jnp.stack([me, plane]), places]).astype(jnp.int32)
    project_meta = expert_meta[1:]
    turn_meta = jnp.concatenate([lengths, (me * span)[None]]).astype(jnp.int32)

    order = list(range(zs))

    def move(x, sender=False, **offset):
        return lax.ppermute(x, "ep", (send_to if sender else fetch_from)(ep, **offset))

    def steps(t):
        n = len(order)
        return t < n - 1, t < n, 1 <= t <= n, 2 <= t < n + 2

    columns, near, far, carried, x = [hidden], {}, {}, None, hidden
    wo_part = [attention_output_weight]
    for t in range(len(order) + 2):
        on_z, on_y, on_core, on_work = steps(t)
        z_new = [move(columns[t], dz=1)] if on_z else []
        y_new = [move(columns[t], dy=k) for k in range(1, ys)] if on_y else []
        c_new = [move(block, dc=1) for block in near[t - 1]] if on_core else []
        if on_work:
            d = order[t - 2]
            carried = project(
                project_meta, near[t - 2] + far[t - 2], head_w, gain_one, cos, sin, zs, d, carried
            )
        block = wo_part[0]
        wo_new = []
        if t == zs - 1:
            wo_new = [move(block, dz=k) for k in range(1, zs)]
        elif t == zs:
            wo_new = [move(block, dy=k) for k in range(1, ys)]
        x, columns, near, far, z_new, y_new, c_new, carried, wo_part, wo_new = phase_tree(
            x, columns, near, far, z_new, y_new, c_new, carried, wo_part, wo_new
        )
        if wo_new:
            wo_part = [jnp.stack(wo_part + wo_new)]
        columns = columns + z_new
        if on_y:
            near[t] = [columns[t]] + y_new
        if on_core:
            far[t - 1] = c_new
        if t == 2:
            upstream = lax.all_gather(phase(lifted, columns[-1])[0], "ep", axis=0)
    wo_new = [
        lax.ppermute(wo_part[0], "dp", [((i + k) % dp, i) for i in range(dp)]) for k in range(1, dp)
    ]
    normed_all, qkv = carried
    made, qk, v, qkt, stat = attend(attend_meta, qkv, seqs, replicas)
    made, wo_new, wo_part = phase_tree(made, wo_new, wo_part)
    recv = lax.all_to_all(made, "ep", split_axis=0, concat_axis=0, tiled=True)
    wo_part = jnp.stack(wo_part + wo_new)
    wo_part = [jnp.stack([wo_part, move(wo_part, dc=1)])]
    line = jnp.arange(dp * ep, dtype=jnp.int32)
    away = (line % 2 - core) % 2
    away = away * dp + (line // ep - lax.axis_index("dp")) % dp
    away = away * ys + ((line // 2) % ys - col) % ys
    away = away * zs + ((line // place) % zs - plane) % zs
    wo = wo_part[0].reshape(dp * ep, own_rows, width)
    wo = jnp.take(wo, away, axis=0, mode="clip").reshape(heads * HD, width)
    if replicas > 1:
        recv = recv.reshape((heads, replicas) + recv.shape[1:]).sum(axis=1).astype(bf16)
    res, pay, mixed, gates = middle(seqs, recv, hidden, wo, gain_two, wr, code)

    count = zs
    columns, near, far, chips, totals = [pay], {}, {}, {}, {}
    outs, carried, extra, passed = {}, None, {}, None
    rings = [[(i, (i + d) % dp) for i in range(dp)] for d in range(1, dp)]
    cuts = ((1,), tuple(range(2, zs)), (0,))

    def hop(value):
        return lax.ppermute(value, "ep", fetch_from(ep, dz=1))

    def swap(piece):
        return [lax.ppermute(piece, "dp", ring) for ring in rings]

    for t in range(count + 5):
        on_z, on_y, on_core, on_work = steps(t)
        z_new = [move(columns[t], dz=1)] if on_z else []
        y_new = [move(columns[t], dy=k) for k in range(1, ys)] if on_y else []
        c_new = [move(block, dc=1) for block in near[t - 1]] if on_core else []
        rc, ry, rz = t - 3, t - 4, t - 5
        rc_new = [move(outs[rc][1], True, dc=1)] if 0 <= rc < count else []
        ry_new = [move(chips[ry][d], True, dy=d) for d in range(1, ys)] if 0 <= ry < count else []
        rz_new = []
        if 1 <= rz < count:
            rz_new = [hop(totals[rz] if rz == 1 else add_low(totals[rz], passed))]
        new = {}
        if on_work:
            d = order[t - 2]
            out = experts(
                expert_meta,
                near[t - 2] + far[t - 2],
                upstream,
                w_gate_up[0],
                w_down[0],
                wr,
                cap,
                zs,
                d,
                carried,
            )
            outs[t - 2], carried = out[:2], out[2:]
        if t == count + 2:
            new["got"] = move(carried[1], True, dc=1)
            new["grads"] = list(expert_grads(carried[2], carried[5], carried[4], carried[3]))
        if t == count + 3:
            new["chip"] = [
                [
                    add_low(
                        jnp.stack([carried[0][k, d] for k in cut]),
                        jnp.stack([extra["got"][k, d] for k in cut]),
                    )
                    for cut in cuts
                    if cut
                ]
                for d in range(ys)
            ]
        if t == count + 4:
            new["swap"] = swap(extra["grads"][0])
            new["first"] = [move(extra["chip"][d][0], True, dy=d) for d in range(1, ys)]
        state = (pay, columns, near, far, outs, chips, totals, carried, extra)
        state = phase_tree(state, z_new, y_new, c_new, rc_new, ry_new, rz_new, new)
        state, z_new, y_new, c_new, rc_new, ry_new, rz_new, new = state
        pay, columns, near, far, outs, chips, totals, carried, extra = state
        columns = columns + z_new
        if on_y:
            near[t] = [columns[t]] + y_new
        if on_core:
            far[t - 1] = c_new
        if rc_new:
            chips[rc] = [add_low(outs[rc][0][d], rc_new[0][d]) for d in range(ys)]
        if 0 <= ry < count:
            totals[ry] = add_low(chips[ry][0], *ry_new)
        if rz_new:
            passed = rz_new[0]
        extra.update(new)
    parts = [totals[0]] + ([passed] if zs > 1 else [])
    moe_chip = extra["chip"]
    grads_low = extra["grads"]

    res_grad, branch, grads, logit_grad, gain_two_grad = turn(
        turn_meta, seqs, parts, res, out_grad, gates, code, wr, gain_two, wo
    )
    if replicas > 1:
        grads = jnp.repeat(grads, replicas, axis=0)
    grads = lax.all_to_all(grads, "ep", split_axis=0, concat_axis=0, tiled=True)
    late = late_grads(expert_count, mixed, branch, pay, logit_grad, gain_two_grad)
    late = late.reshape(dp, zs * ys, 2, own_rows, late.shape[1])

    def stage_parts(value, axis, here_at, size):
        return [
            lax.dynamic_index_in_dim(value, (here_at + d) % size, axis, keepdims=False)
            for d in range(size)
        ]

    late_parts = stage_parts(late, 2, core, 2)
    moe = [add_low(moe_chip[0][0], *extra["first"])]
    moe_new = [move(moe_chip[d][1], True, dy=d) for d in range(1, ys)]
    grads_moved = [extra["swap"], swap(grads_low[1])]
    state = (grads, moe, moe_new, moe_chip, late_parts, grads_low, grads_moved)
    grads, moe, moe_new, moe_chip, late_parts, grads_low, grads_moved = phase_tree(*state)
    moe.append(add_low(moe_chip[0][1], *moe_new))

    dqkv = back(attend_meta, grads, qk, v, qkt, stat, cos, sin, qkv.shape, seqs, replicas)
    moe_new = [move(moe_chip[d][2], True, dy=d) for d in range(1, ys)]
    passed = hop(moe[0][0])
    late_got = [move(late_parts[1], True, dc=1)]
    swapped = swap(grads_low[2])
    state = (dqkv, moe, moe_new, passed, moe_chip, late_parts, late_got, grads_low, swapped)
    state = phase_tree(*state)
    dqkv, moe, moe_new, passed, moe_chip, late_parts, late_got, grads_low, swapped = state
    moe.append(add_low(moe_chip[0][2], *moe_new))
    grads_moved.append(swapped)
    late = add_low(late_parts[0], *late_got)
    late_parts = stage_parts(late, 0, lax.axis_index("dp"), dp)
    late_got = [lax.ppermute(part, "dp", ring) for part, ring in zip(late_parts[1:], rings)]

    halves = ((1, 2), (3, 0)) if zs == 4 else (tuple(range(1, zs)), (0,))
    turn_order = [d for half in halves for d in half]
    near, far = ([part] for part in spread(dqkv, head_w, halves[0]))
    near, far, dqkv = phase_tree(near, far, dqkv)

    got = [move(far[0], True, dc=1)]
    more = spread(dqkv, head_w, halves[1])
    near.append(more[0])
    far.append(more[1])
    passed = hop(add_low(moe[1][0], passed))
    head_grad = head_grads(dqkv, normed_all).reshape(dp * ep, own_rows, PACK)
    state = (near, far, got, moe, passed, head_grad, late_parts, late_got, grads_low)
    near, far, got, moe, passed, head_grad, late_parts, late_got, grads_low = phase_tree(*state)
    late = add_low(late_parts[0], *late_got)
    plane_groups = [[c + 2 * k for k in range(zs * ys)] for c in range(2)]
    late = lax.all_to_all(
        late, "ep", split_axis=0, concat_axis=0, tiled=True, axis_index_groups=plane_groups
    )

    head_grad = lax.all_to_all(head_grad, ("dp", "ep"), split_axis=0, concat_axis=0, tiled=True)
    totals, received = {}, None

    def chip_of(d):
        half = 0 if d in halves[0] else 1
        at = halves[half].index(d)
        return [add_low(near[half][at, y], got[half][at, y]) for y in range(ys)]

    chip = chip_of(turn_order[0])
    for k, d in enumerate(turn_order):
        ahead = chip_of(turn_order[k + 1]) if k + 1 < len(turn_order) else []
        moved = [move(chip[y], True, dy=y) for y in range(1, ys)]
        if k:
            last = totals[turn_order[k - 1]]
            received = hop(last if k == 1 else add_low(last, received))
        if k == 0:
            got.append(move(far[1], True, dc=1))
            passed = hop(add_low(moe[1][1], passed)) if zs == 4 else passed
            swapped = swap(grads_low[3])
            near, got, chip, ahead, moved, passed, swapped = phase_tree(
                near, got, chip, ahead, moved, passed, swapped
            )
            grads_moved.append(swapped)
        elif k == 2:
            near, got, chip, ahead, moved, received, totals, head_grad = phase_tree(
                near, got, chip, ahead, moved, received, totals, head_grad
            )
        else:
            near, got, chip, ahead, moved, received, totals = phase_tree(
                near, got, chip, ahead, moved, received, totals
            )
        totals[d] = add_low(chip[0], *moved)
        chip = ahead
    parts = [totals[0], received]
    late = phase(late, totals[0], received)[0]
    late = late.astype(f32).sum(axis=0)
    mparts = [moe[-1][0], passed]
    sums = []
    for own, moved in zip(grads_low, grads_moved):
        piece = own.astype(f32)
        for other in moved:
            piece = piece + other.astype(f32)
        sums.append(piece)
    grads_total = jnp.concatenate(sums)
    gu_total = grads_total[0:width]
    d_total = grads_total[width:]

    head_grad = head_grad.astype(f32).reshape(dp, heads, replicas, own_rows, PACK).sum(axis=(0, 2))

    def rows_of(part, count):
        part = part.reshape(count, heads // count, own_rows, HD).sum(axis=1)
        return part.transpose(1, 0, 2).reshape(own_rows, count * HD)

    query_w_grad = rows_of(head_grad[..., 0:HD], heads)
    key_w_grad = rows_of(head_grad[..., HD : 2 * HD], kv_heads)
    value_w_grad = rows_of(head_grad[..., 2 * HD : 3 * HD], kv_heads)
    gain_one_grad = (
        jnp.sum(query_w_grad * query_weight_matrix.astype(f32), axis=1)
        + jnp.sum(key_w_grad * key_weight_matrix.astype(f32), axis=1)
        + jnp.sum(value_w_grad * value_weight_matrix.astype(f32), axis=1)
    ) / attn_gain.astype(f32)

    moe_own = res
    for part in mparts:
        moe_own = moe_own + part.astype(f32)
    output = jnp.where(
        is_valid[..., None], moe_own.reshape(seqs, span, width), 0.0
    ).astype(bf16)
    input_grad = finish(hidden, gain_one, res_grad, parts)
    model = width
    return (
        output,
        input_grad.reshape(seqs, span, width),
        gain_one_grad,
        query_w_grad,
        key_w_grad,
        value_w_grad,
        late[:, 0:model],
        late[:, model + expert_count],
        late[:, model : model + expert_count],
        gu_total[None],
        d_total[None],
    )


def solution(mesh):
    return jax.shard_map(
        body,
        mesh=mesh,
        in_specs=(
            P("dp", "ep", None),
            P("dp"),
            P("dp", "ep", None),
            P("dp", "ep", None),
            P(("dp", "ep")),
            P(("dp", "ep"), None),
            P(("dp", "ep"), None),
            P(("dp", "ep"), None),
            P(("dp", "ep"), None),
            P(("dp", "ep")),
            P(("dp", "ep"), None),
            P("ep", None, None),
            P("ep", None, None),
            P("dp", "ep", None),
        ),
        out_specs=(
            P("dp", "ep", None),
            P("dp", "ep", None),
            P(("dp", "ep")),
            P(("dp", "ep"), None),
            P(("dp", "ep"), None),
            P(("dp", "ep"), None),
            P(("dp", "ep"), None),
            P(("dp", "ep")),
            P(("dp", "ep"), None),
            P("ep", None, None),
            P("ep", None, None),
        ),
        check_vma=False,
    )
```

profile of v0, /device:TPU:8, one launch (start us, length us, event | category | flops | bytes accessed | tf_op | source)
XLA Modules:
  0.0 500.4 jit_solution(15872757268696342381)
XLA Ops:
  14.1 5.9 %all-to-all-start = ((bf16[32,32,256]{2,1,0:T(8,128)(2,1)}), bf16[32,32,256]{2,1,0:T(8,128)(2,1)S(1)}, u32[]{:S(2)}, u32[]{:S(2)}) async-start(bf16[32,32,256]{2,1,0:T(8,128)(2,1)} %bitcast.9), calls=%async_computation | async-start | bytes 1048576 | tf_op jit(solution)/shard_map/all_to_all | solution.py:923
  35.3 11.2 %collective-permute-done.2.refs_0_ = bf16[288,1024]{1,0:T(8,128)(2,1)S(1)} collective-permute-done((bf16[288,1024]{1,0:T(8,128)(2,1)}, bf16[288,1024]{1,0:T(8,128)(2,1)S(1)}, u32[]{:S(2)}, u32[]{:S(2)}) %collective-permute-start.2) | collective-permute-done | bytes 589856 | tf_op jit(solution)/shard_map/ppermute | solution.py:966
  53.3 5.5 %project_in.4 = (bf16[4,4,288,1024]{3,2,1,0:T(8,128)(2,1)}, bf16[4,4,288,256]{3,2,1,0:T(8,128)(2,1)}) custom-call(s32[5]{0:T(128)} %pad_add_fusion.meta, bf16[288,1024]{1,0:T(8,128)(2,1)} %bitcast.161, bf16[288,1024]{1,0:T(8,128)(2,1)} %collective-permute-done.1.refs_1_, bf16[288,1024]{1,0:T(8,128)(2,1)} %collective-permute-done.4.refs_2_, ...), custom_call_target="tpu_custom_call" | custom-call | flops 603979776 | bytes 4718592 | tf_op jit(solution)/shard_map/project_in/pallas_call | solution.py:119
  71.6 5.6 %project_in.5 = (bf16[4,4,288,1024]{3,2,1,0:T(8,128)(2,1)}, bf16[4,4,288,256]{3,2,1,0:T(8,128)(2,1)}) custom-call(s32[5]{0:T(128)} %pad_add_fusion.meta, bf16[288,1024]{1,0:T(8,128)(2,1)} %collective-permute-done.refs_0_, bf16[288,1024]{1,0:T(8,128)(2,1)} %collective-permute-done.3.refs_1_, ...), custom_call_target="tpu_custom_call", output_to_operand_aliasing={{0}: (9, {}), {1}: (10, {})} | custom-call | flops 603979776 | bytes 4718592 | tf_op jit(solution)/shard_map/project_in/pallas_call | solution.py:119
  81.3 5.4 %project_in.6 = (bf16[4,4,288,1024]{3,2,1,0:T(8,128)(2,1)}, bf16[4,4,288,256]{3,2,1,0:T(8,128)(2,1)}) custom-call(s32[5]{0:T(128)} %pad_add_fusion.meta, bf16[288,1024]{1,0:T(8,128)(2,1)} %copy-done.18, bf16[288,1024]{1,0:T(8,128)(2,1)} %copy-done.20, bf16[288,1024]{1,0:T(8,128)(2,1)} %copy-done.25, ...), custom_call_target="tpu_custom_call", output_to_operand_aliasing={{0}: (9, {}), {1}: (10, {})} | custom-call | flops 603979776 | bytes 4718592 | tf_op jit(solution)/shard_map/project_in/pallas_call | solution.py:119
  89.5 5.4 %project_in.7 = (bf16[4,4,288,1024]{3,2,1,0:T(8,128)(2,1)}, bf16[4,4,288,256]{3,2,1,0:T(8,128)(2,1)}) custom-call(s32[5]{0:T(128)} %pad_add_fusion.meta, bf16[288,1024]{1,0:T(8,128)(2,1)} %copy-done.19, bf16[288,1024]{1,0:T(8,128)(2,1)} %copy-done.21, bf16[288,1024]{1,0:T(8,128)(2,1)} %copy-done.28, ...), custom_call_target="tpu_custom_call", output_to_operand_aliasing={{0}: (9, {}), {1}: (10, {})} | custom-call | flops 603979776 | bytes 4718592 | tf_op jit(solution)/shard_map/project_in/pallas_call | solution.py:119
  97.1 11.2 %attend_forward.1 = (bf16[16,144,128]{2,1,0:T(8,128)(2,1)}, bf16[3,1536,128]{2,1,0:T(8,128)(2,1)}, bf16[3,1536,128]{2,1,0:T(8,128)(2,1)}, bf16[3,128,1536]{2,1,0:T(8,128)(2,1)}, f32[3,72,1536]{2,1,0:T(8,128)}) custom-call(s32[12]{0:T(128)} %concatenate.34.meta, bf16[4,4,288,256]{3,2,1,0:T(8,128)(2,1)} %get-tuple-element.358.qkv_ref), custom_call_target="tpu_custom_call" | custom-call | flops 3623878656 | bytes 4718592 | tf_op jit(solution)/shard_map/attend_forward/pallas_call | solution.py:220
  110.9 9.8 %all-to-all-start.1 = ((bf16[16,144,128]{2,1,0:T(8,128)(2,1)}), bf16[16,144,128]{2,1,0:T(8,128)(2,1)}, u32[]{:S(2)}, u32[]{:S(2)}) async-start(bf16[16,144,128]{2,1,0:T(8,128)(2,1)} %get-tuple-element.361), calls=%async_computation.1 | async-start | bytes 1179648 | tf_op jit(solution)/shard_map/all_to_all | solution.py:1008
  125.1 24.2 %all-to-all-done.1.recv_ref = bf16[16,144,128]{2,1,0:T(8,128)(2,1)} async-done(((bf16[16,144,128]{2,1,0:T(8,128)(2,1)}), bf16[16,144,128]{2,1,0:T(8,128)(2,1)}, u32[]{:S(2)}, u32[]{:S(2)}) %all-to-all-start.1) | async-done | bytes 589856 | tf_op jit(solution)/shard_map/all_to_all | solution.py:1008
  149.2 4.5 project_out.1
  157.5 13.0 %collective-permute-done.21.refs_0_ = bf16[288,1024]{1,0:T(8,128)(2,1)S(1)} collective-permute-done((bf16[288,1024]{1,0:T(8,128)(2,1)}, bf16[288,1024]{1,0:T(8,128)(2,1)S(1)}, u32[]{:S(2)}, u32[]{:S(2)}) %collective-permute-start.21) | collective-permute-done | bytes 589856 | tf_op jit(solution)/shard_map/ppermute | solution.py:966
  175.9 10.6 %collective-permute-done.23.refs_0_ = bf16[288,1024]{1,0:T(8,128)(2,1)S(1)} collective-permute-done((bf16[288,1024]{1,0:T(8,128)(2,1)S(1)}, bf16[288,1024]{1,0:T(8,128)(2,1)S(1)}, u32[]{:S(2)}, u32[]{:S(2)}) %collective-permute-start.23) | collective-permute-done | bytes 589856 | tf_op jit(solution)/shard_map/ppermute | solution.py:966
  194.9 12.1 %experts.4 = (bf16[2,304,1024]{2,1,0:T(8,128)(2,1)}, bf16[2,304,1024]{2,1,0:T(8,128)(2,1)}, bf16[4,2,288,1024]{3,2,1,0:T(8,128)(2,1)}, bf16[4,2,288,1024]{3,2,1,...) custom-call(s32[6]{0:T(128)} %pad_add_fusion.2.meta, ...), custom_call_target="tpu_custom_call" | custom-call | flops 4831838208 | bytes 7077888 | tf_op jit(solution)/shard_map/experts/pallas_call | solution.py:456
  209.0 12.4 %experts.5 = (bf16[2,304,1024]{2,1,0:T(8,128)(2,1)}, bf16[2,304,1024]{2,1,0:T(8,128)(2,1)}, bf16[4,2,288,1024]{3,2,1,0:T(8,128)(2,1)}, bf16[4,2,288,1024]{3,2,1,...) custom-call(s32[6]{0:T(128)} %pad_add_fusion.2.meta, ...), custom_call_target="tpu_custom_call", output_to_operand_aliasing={{2}: (9, {}), {3}: (10, {}), {4}: (11, {}), {5}: (12, {}), ... | custom-call | flops 4831838208 | bytes 7077888 | tf_op jit(solution)/shard_map/experts/pallas_call | solution.py:456
  226.4 12.2 %experts.6 = (bf16[2,304,1024]{2,1,0:T(8,128)(2,1)}, bf16[2,304,1024]{2,1,0:T(8,128)(2,1)}, bf16[4,2,288,1024]{3,2,1,0:T(8,128)(2,1)}, bf16[4,2,288,1024]{3,2,1,...) custom-call(s32[6]{0:T(128)} %pad_add_fusion.2.meta, ...), custom_call_target="tpu_custom_call", output_to_operand_aliasing={{2}: (9, {}), {3}: (10, {}), {4}: (11, {}), {5}: (12, {}), ... | custom-call | flops 4831838208 | bytes 7077888 | tf_op jit(solution)/shard_map/experts/pallas_call | solution.py:456
  244.5 12.3 %experts.7 = (bf16[2,304,1024]{2,1,0:T(8,128)(2,1)}, bf16[2,304,1024]{2,1,0:T(8,128)(2,1)}, bf16[4,2,288,1024]{3,2,1,0:T(8,128)(2,1)}, bf16[4,2,288,1024]{3,2,1,...) custom-call(s32[6]{0:T(128)} %pad_add_fusion.2.meta, ...), custom_call_target="tpu_custom_call", output_to_operand_aliasing={{2}: (9, {}), {3}: (10, {}), {4}: (11, {}), {5}: (12, {}), ... | custom-call | flops 4831838208 | bytes 7077888 | tf_op jit(solution)/shard_map/experts/pallas_call | solution.py:456
  266.3 15.3 %expert_grads.1 = (bf16[384,1024]{1,0:T(8,128)(2,1)}, bf16[384,1024]{1,0:T(8,128)(2,1)}, bf16[384,1024]{1,0:T(8,128)(2,1)}, bf16[384,1024]{1,0:T(8,128)(2,1)}) custom-call(bf16[4,576,1024]{2,1,0:T(8,128)(2,1)} %get-tuple-element.471.x_ref, bf16[4,576,1024]{2,1,0:T(8,128)(2,1)} %get-tuple-element.474.both_ref, ...), custom_call_target="tpu_custom_call" | custom-call | flops 7247757312 | bytes 18874368 | tf_op jit(solution)/shard_map/expert_grads/pallas_call | solution.py:729
  304.1 11.0 %collective-permute-done.48 = bf16[1,288,1024]{2,1,0:T(8,128)(2,1)S(1)} collective-permute-done((bf16[1,288,1024]{2,1,0:T(8,128)(2,1)S(1)}, bf16[1,288,1024]{2,1,0:T(8,128)(2,1)S(1)}, u32[]{:S(2)}, u32[]{:S(2)}) %collective-permute-start.48) | collective-permute-done | bytes 589856 | tf_op jit(solution)/shard_map/ppermute | solution.py:966
  319.7 6.1 %turn_back.1 = (f32[288,1024]{1,0:T(8,128)}, bf16[288,1024]{1,0:T(8,128)(2,1)}, bf16[16,144,128]{2,1,0:T(8,128)(2,1)}, f32[288,128]{1,0:T(8,128)}, f32[1,1024]{1,0:T(1,128)}) custom-call(s32[4]{0:T(128)} %pad_add_fusion.1.meta, bf16[304,1024]{1,0:T(8,128)(2,1)} %add_convert_fusion.13.refs_0_, bf16[304,1024]{1,0:T(8,128)(2,1)} %copy-done.17, ...), custom_call_target="tpu_custom_call" | custom-call | flops 1207959552 | bytes 4194304 | tf_op jit(solution)/shard_map/turn_back/pallas_call | solution.py:562
  325.8 6.5 %all-to-all-start.2 = ((bf16[16,144,128]{2,1,0:T(8,128)(2,1)}), bf16[16,144,128]{2,1,0:T(8,128)(2,1)}, u32[]{:S(2)}, u32[]{:S(2)}) async-start(bf16[16,144,128]{2,1,0:T(8,128)(2,1)} %get-tuple-element.510), calls=%async_computation.2 | async-start | bytes 1179648 | tf_op jit(solution)/shard_map/all_to_all | solution.py:1104
  332.8 4.6 late_grads.1
  341.3 11.0 %collective-permute-done.51 = bf16[384,1024]{1,0:T(8,128)(2,1)} collective-permute-done((bf16[384,1024]{1,0:T(8,128)(2,1)}, bf16[384,1024]{1,0:T(8,128)(2,1)}, u32[]{:S(2)}, u32[]{:S(2)}) %collective-permute-start.51) | collective-permute-done | bytes 786464 | tf_op jit(solution)/shard_map/ppermute | solution.py:1032
  356.7 17.6 %attend_backward.1.dqkv_ref = bf16[4,4,288,256]{3,2,1,0:T(8,128)(2,1)} custom-call(s32[12]{0:T(128)} %concatenate.34.meta, bf16[16,144,128]{2,1,0:T(8,128)(2,1)} %all-to-all-done.2.grad_ref, bf16[3,1536,128]{2,1,0:T(8,128)(2,1)} %get-tuple-element.528.qk_ref, bf16[3,1536,128]{2,1,0:T(8,128)(2,1)} %get-tuple-element.529.v_ref, ...), custom_call_target="tpu_custom_call" | custom-call | flops 9059696640 | bytes 7077888 | tf_op jit(solution)/shard_map/attend_backward/pallas_call | solution.py:671
  374.4 4.9 spread.2
  386.9 4.0 spread.3
  390.9 7.8 %head_grads.1 = bf16[1024,256]{1,0:T(8,128)(2,1)} custom-call(bf16[4,4,288,256]{3,2,1,0:T(8,128)(2,1)} %attend_backward.1.dqkv_ref, bf16[4,4,288,1024]{3,2,1,0:T(8,128)(2,1)} %get-tuple-element.555.normed_ref), custom_call_target="tpu_custom_call" | custom-call | flops 2415919104 | bytes 9437184 | tf_op jit(solution)/shard_map/head_grads/pallas_call | solution.py:789
  408.4 5.2 %all-to-all-start.3 = ((bf16[32,32,256]{2,1,0:T(8,128)(2,1)}), bf16[32,32,256]{2,1,0:T(8,128)(2,1)}, u32[]{:S(2)}, u32[]{:S(2)}) async-start(bf16[32,32,256]{2,1,0:T(8,128)(2,1)} %bitcast.165), calls=%async_computation.3 | async-start | bytes 1048576 | tf_op jit(solution)/shard_map/all_to_all | solution.py:1155
  421.0 4.3 collective-permute-done.61
  425.2 4.5 collective-permute-done.62
  453.9 5.5 %all-to-all-start.4 = ((bf16[8,32,1152]{2,1,0:T(8,128)(2,1)}), bf16[8,32,1152]{2,1,0:T(8,128)(2,1)S(1)}, u32[]{:S(2)}, u32[]{:S(2)}) async-start(bf16[8,32,1152]{2,1,0:T(8,128)(2,1)} %add_convert_fusion.18), calls=%async_computation.4 | async-start | bytes 1179648 | tf_op jit(solution)/shard_map/all_to_all | solution.py:1151
  460.9 7.6 %collective-permute-done.66 = bf16[288,1024]{1,0:T(8,128)(2,1)} collective-permute-done((bf16[288,1024]{1,0:T(8,128)(2,1)}, bf16[288,1024]{1,0:T(8,128)(2,1)}, u32[]{:S(2)}, u32[]{:S(2)}) %collective-permute-start.66) | collective-permute-done | bytes 589856 | tf_op jit(solution)/shard_map/ppermute | solution.py:1029
  479.7 6.9 %collective-permute-done.68.refs_4_ = bf16[288,1024]{1,0:T(8,128)(2,1)S(1)} collective-permute-done((bf16[288,1024]{1,0:T(8,128)(2,1)}, bf16[288,1024]{1,0:T(8,128)(2,1)S(1)}, u32[]{:S(2)}, u32[]{:S(2)}) %collective-permute-start.68) | collective-permute-done | bytes 589856 | tf_op jit(solution)/shard_map/ppermute | solution.py:1029
  (364 shorter events, 201.3 us)
Async XLA Ops:
  7.2 22.5 %collective-permute-start = (bf16[288,1024]{1,0:T(8,128)(2,1)}, bf16[288,1024]{1,0:T(8,128)(2,1)}, u32[]{:S(2)}, u32[]{:S(2)}) collective-permute-start(bf16[288,1024]{1,0:T(8,128)(2,1)} %bitcast.158), channel_id=1, source_target_pairs={{4,0},{5,1},{6,2},{7,3},{8,4},{9,5},{10,6},{11,7},{12,8},{13,9},{1... | collective-permute-start | bytes 1769480 | tf_op jit(solution)/shard_map/ppermute | solution.py:966
  7.2 22.4 %collective-permute-start.1 = (bf16[288,1024]{1,0:T(8,128)(2,1)}, bf16[288,1024]{1,0:T(8,128)(2,1)}, u32[]{:S(2)}, u32[]{:S(2)}) collective-permute-start(bf16[288,1024]{1,0:T(8,128)(2,1)} %bitcast.159), channel_id=1, source_target_pairs={{2,0},{3,1},{0,2},{1,3},{6,4},{7,5},{4,6},{5,7},{10,8},{11,9},{8,1... | collective-permute-start | bytes 1769480 | tf_op jit(solution)/shard_map/ppermute | solution.py:966
  14.1 37.0 %all-to-all-start = ((bf16[32,32,256]{2,1,0:T(8,128)(2,1)}), bf16[32,32,256]{2,1,0:T(8,128)(2,1)S(1)}, u32[]{:S(2)}, u32[]{:S(2)}) async-start(bf16[32,32,256]{2,1,0:T(8,128)(2,1)} %bitcast.9), calls=%async_computation | async-start | bytes 1048576 | tf_op jit(solution)/shard_map/all_to_all | solution.py:923
  20.0 174.8 %all-gather.3.cloned.1.call-start = ((), (), s32[]{:S(2)}) async-start(), calls=%async_computation.5 | async-start | bytes 10584064 | tf_op jit(solution)/shard_map/all_gather | solution.py:1001
  29.7 16.8 %collective-permute-start.2 = (bf16[288,1024]{1,0:T(8,128)(2,1)}, bf16[288,1024]{1,0:T(8,128)(2,1)S(1)}, u32[]{:S(2)}, u32[]{:S(2)}) collective-permute-start(bf16[288,1024]{1,0:T(8,128)(2,1)} %collective-permute-done.refs_0_), channel_id=1, source_target_pairs={{4,0},{5,1},{6,2},{7,3},{8,4},{9,5},{10,6},{11,7},{12,8},{13,9},{1... | collective-permute-start | bytes 1769480 | tf_op jit(solution)/shard_map/ppermute | solution.py:966
  110.9 38.3 %all-to-all-start.1 = ((bf16[16,144,128]{2,1,0:T(8,128)(2,1)}), bf16[16,144,128]{2,1,0:T(8,128)(2,1)}, u32[]{:S(2)}, u32[]{:S(2)}) async-start(bf16[16,144,128]{2,1,0:T(8,128)(2,1)} %get-tuple-element.361), calls=%async_computation.1 | async-start | bytes 1179648 | tf_op jit(solution)/shard_map/all_to_all | solution.py:1008
  153.7 16.8 %collective-permute-start.21 = (bf16[288,1024]{1,0:T(8,128)(2,1)}, bf16[288,1024]{1,0:T(8,128)(2,1)S(1)}, u32[]{:S(2)}, u32[]{:S(2)}) collective-permute-start(bf16[288,1024]{1,0:T(8,128)(2,1)} %get-tuple-element.519.refs_0_.pay_ref), channel_id=1, source_target_pairs={{4,0},{5,1},{6,2},{7,3},{8,4},{9,5},{10,6},{11,7},{12,8},{13,9},{1... | collective-permute-start | bytes 1769480 | tf_op jit(solution)/shard_map/ppermute | solution.py:966
  153.7 17.7 %collective-permute-start.22 = (bf16[288,1024]{1,0:T(8,128)(2,1)}, bf16[288,1024]{1,0:T(8,128)(2,1)S(1)}, u32[]{:S(2)}, u32[]{:S(2)}) collective-permute-start(bf16[288,1024]{1,0:T(8,128)(2,1)} %get-tuple-element.519.refs_0_.pay_ref), channel_id=1, source_target_pairs={{2,0},{3,1},{0,2},{1,3},{6,4},{7,5},{4,6},{5,7},{10,8},{11,9},{8,1... | collective-permute-start | bytes 1769480 | tf_op jit(solution)/shard_map/ppermute | solution.py:966
  189.9 17.1 %collective-permute-start.27 = (bf16[288,1024]{1,0:T(8,128)(2,1)S(1)}, bf16[288,1024]{1,0:T(8,128)(2,1)S(1)}, u32[]{:S(2)}, u32[]{:S(2)}) collective-permute-start(bf16[288,1024]{1,0:T(8,128)(2,1)S(1)} %collective-permute-done.23.refs_0_), channel_id=1, source_target_pairs={{4,0},{5,1},{6,2},{7,3},{8,4},{9,5},{10,6},{11,7},{12,8},{13,9},{1... | collective-permute-start | bytes 1769480 | tf_op jit(solution)/shard_map/ppermute | solution.py:966
  224.0 17.0 %collective-permute-start.37 = (bf16[2,304,1024]{2,1,0:T(8,128)(2,1)}, bf16[2,304,1024]{2,1,0:T(8,128)(2,1)S(1)}, u32[]{:S(2)}, u32[]{:S(2)}) collective-permute-start(bf16[2,304,1024]{2,1,0:T(8,128)(2,1)} %get-tuple-element.420), channel_id=1, source_target_pairs={{0,1},{1,0},{2,3},{3,2},{4,5},{5,4},{6,7},{7,6},{8,9},{9,8},{10,11... | collective-permute-start | bytes 3735560 | tf_op jit(solution)/shard_map/ppermute | solution.py:966
  224.5 16.5 %collective-permute-start.38 = (bf16[304,1024]{1,0:T(8,128)(2,1)S(1)}, bf16[304,1024]{1,0:T(8,128)(2,1)S(1)}, u32[]{:S(2)}, u32[]{:S(2)}) collective-permute-start(bf16[304,1024]{1,0:T(8,128)(2,1)S(1)} %get-tuple-element.733), channel_id=1, source_target_pairs={{0,2},{1,3},{2,0},{3,1},{4,6},{5,7},{6,4},{7,5},{8,10},{9,11},{10,... | collective-permute-start | bytes 1867784 | tf_op jit(solution)/shard_map/ppermute | solution.py:966
  241.0 17.5 %collective-permute-start.39 = (bf16[2,304,1024]{2,1,0:T(8,128)(2,1)}, bf16[2,304,1024]{2,1,0:T(8,128)(2,1)S(1)}, u32[]{:S(2)}, u32[]{:S(2)}) collective-permute-start(bf16[2,304,1024]{2,1,0:T(8,128)(2,1)} %get-tuple-element.443), channel_id=1, source_target_pairs={{0,1},{1,0},{2,3},{3,2},{4,5},{5,4},{6,7},{7,6},{8,9},{9,8},{10,11... | collective-permute-start | bytes 3735560 | tf_op jit(solution)/shard_map/ppermute | solution.py:966
  258.5 23.1 %collective-permute-start.44 = (bf16[4,2,288,1024]{3,2,1,0:T(8,128)(2,1)}, bf16[4,2,288,1024]{3,2,1,0:T(8,128)(2,1)}, u32[]{:S(2)}, u32[]{:S(2)}) collective-permute-start(bf16[4,2,288,1024]{3,2,1,0:T(8,128)(2,1)} %get-tuple-element.470), channel_id=1, source_target_pairs={{0,1},{1,0},{2,3},{3,2},{4,5},{5,4},{6,7},{7,6},{8,9},{9,8},{10,11... | collective-permute-start | bytes 14155784 | tf_op jit(solution)/shard_map/ppermute | solution.py:966
  258.5 23.1 %collective-permute-start.41 = (bf16[2,304,1024]{2,1,0:T(8,128)(2,1)}, bf16[2,304,1024]{2,1,0:T(8,128)(2,1)S(1)}, u32[]{:S(2)}, u32[]{:S(2)}) collective-permute-start(bf16[2,304,1024]{2,1,0:T(8,128)(2,1)} %get-tuple-element.464), channel_id=1, source_target_pairs={{0,1},{1,0},{2,3},{3,2},{4,5},{5,4},{6,7},{7,6},{8,9},{9,8},{10,11... | collective-permute-start | bytes 3735560 | tf_op jit(solution)/shard_map/ppermute | solution.py:966
  260.4 21.2 %collective-permute-start.42 = (bf16[304,1024]{1,0:T(8,128)(2,1)}, bf16[304,1024]{1,0:T(8,128)(2,1)}, u32[]{:S(2)}, u32[]{:S(2)}) collective-permute-start(bf16[304,1024]{1,0:T(8,128)(2,1)} %get-tuple-element.729), channel_id=1, source_target_pairs={{0,2},{1,3},{2,0},{3,1},{4,6},{5,7},{6,4},{7,5},{8,10},{9,11},{10,... | collective-permute-start | bytes 1867784 | tf_op jit(solution)/shard_map/ppermute | solution.py:966
  264.0 17.6 %collective-permute-start.43 = (bf16[304,1024]{1,0:T(8,128)(2,1)}, bf16[304,1024]{1,0:T(8,128)(2,1)}, u32[]{:S(2)}, u32[]{:S(2)}) collective-permute-start(bf16[304,1024]{1,0:T(8,128)(2,1)} %add_convert_fusion.10), channel_id=1, source_target_pairs={{4,0},{5,1},{6,2},{7,3},{8,4},{9,5},{10,6},{11,7},{12,8},{13,9},{1... | collective-permute-start | bytes 1867784 | tf_op jit(solution)/shard_map/ppermute | solution.py:1029
  299.6 17.8 %collective-permute-start.49 = (bf16[384,1024]{1,0:T(8,128)(2,1)S(1)}, bf16[384,1024]{1,0:T(8,128)(2,1)S(1)}, u32[]{:S(2)}, u32[]{:S(2)}) collective-permute-start(bf16[384,1024]{1,0:T(8,128)(2,1)S(1)} %copy-done.11), channel_id=1, source_target_pairs={{0,16},{16,0},{1,17},{17,1},{2,18},{18,2},{3,19},{19,3},{4,20},{20... | collective-permute-start | bytes 2359304 | tf_op jit(solution)/shard_map/ppermute | solution.py:1032
  318.2 34.0 %collective-permute-start.50 = (bf16[2,288,1024]{2,1,0:T(8,128)(2,1)}, bf16[2,288,1024]{2,1,0:T(8,128)(2,1)}, u32[]{:S(2)}, u32[]{:S(2)}) collective-permute-start(bf16[2,288,1024]{2,1,0:T(8,128)(2,1)} %add_convert_fusion.2), channel_id=1, source_target_pairs={{0,2},{1,3},{2,0},{3,1},{4,6},{5,7},{6,4},{7,5},{8,10},{9,11},{10,... | collective-permute-start | bytes 3538952 | tf_op jit(solution)/shard_map/ppermute | solution.py:966
  325.8 26.4 %all-to-all-start.2 = ((bf16[16,144,128]{2,1,0:T(8,128)(2,1)}), bf16[16,144,128]{2,1,0:T(8,128)(2,1)}, u32[]{:S(2)}, u32[]{:S(2)}) async-start(bf16[16,144,128]{2,1,0:T(8,128)(2,1)} %get-tuple-element.510), calls=%async_computation.2 | async-start | bytes 1179648 | tf_op jit(solution)/shard_map/all_to_all | solution.py:1104
  332.3 19.9 %collective-permute-start.51 = (bf16[384,1024]{1,0:T(8,128)(2,1)}, bf16[384,1024]{1,0:T(8,128)(2,1)}, u32[]{:S(2)}, u32[]{:S(2)}) collective-permute-start(bf16[384,1024]{1,0:T(8,128)(2,1)} %get-tuple-element.600), channel_id=1, source_target_pairs={{0,16},{16,0},{1,17},{17,1},{2,18},{18,2},{3,19},{19,3},{4,20},{20... | collective-permute-start | bytes 2359304 | tf_op jit(solution)/shard_map/ppermute | solution.py:1032
  352.2 22.2 %collective-permute-start.54 = (bf16[2,8,32,1152]{3,2,1,0:T(8,128)(2,1)}, bf16[2,8,32,1152]{3,2,1,0:T(8,128)(2,1)S(1)}, u32[]{:S(2)}, u32[]{:S(2)}) collective-permute-start(bf16[2,8,32,1152]{3,2,1,0:T(8,128)(2,1)} %get-tuple-element.538), channel_id=1, source_target_pairs={{0,1},{1,0},{2,3},{3,2},{4,5},{5,4},{6,7},{7,6},{8,9},{9,8},{10,11... | collective-permute-start | bytes 3538952 | tf_op jit(solution)/shard_map/ppermute | solution.py:966
  352.2 22.1 %collective-permute-start.52 = (bf16[1,288,1024]{2,1,0:T(8,128)(2,1)}, bf16[1,288,1024]{2,1,0:T(8,128)(2,1)S(1)}, u32[]{:S(2)}, u32[]{:S(2)}) collective-permute-start(bf16[1,288,1024]{2,1,0:T(8,128)(2,1)} %get-tuple-element.535), channel_id=1, source_target_pairs={{0,2},{1,3},{2,0},{3,1},{4,6},{5,7},{6,4},{7,5},{8,10},{9,11},{10,... | collective-permute-start | bytes 1769480 | tf_op jit(solution)/shard_map/ppermute | solution.py:966
  353.8 20.6 %collective-permute-start.53 = (bf16[288,1024]{1,0:T(8,128)(2,1)}, bf16[288,1024]{1,0:T(8,128)(2,1)S(1)}, u32[]{:S(2)}, u32[]{:S(2)}) collective-permute-start(bf16[288,1024]{1,0:T(8,128)(2,1)} %bitcast.57), channel_id=1, source_target_pairs={{4,0},{5,1},{6,2},{7,3},{8,4},{9,5},{10,6},{11,7},{12,8},{13,9},{1... | collective-permute-start | bytes 1769480 | tf_op jit(solution)/shard_map/ppermute | solution.py:1029
  354.5 19.9 %collective-permute-start.55 = (bf16[384,1024]{1,0:T(8,128)(2,1)}, bf16[384,1024]{1,0:T(8,128)(2,1)S(1)}, u32[]{:S(2)}, u32[]{:S(2)}) collective-permute-start(bf16[384,1024]{1,0:T(8,128)(2,1)} %get-tuple-element.602), channel_id=1, source_target_pairs={{0,16},{16,0},{1,17},{17,1},{2,18},{18,2},{3,19},{19,3},{4,20},{20... | collective-permute-start | bytes 2359304 | tf_op jit(solution)/shard_map/ppermute | solution.py:1032
  379.4 21.4 %collective-permute-start.56 = (bf16[2,2,288,1024]{3,2,1,0:T(8,128)(2,1)}, bf16[2,2,288,1024]{3,2,1,0:T(8,128)(2,1)}, u32[]{:S(2)}, u32[]{:S(2)}) collective-permute-start(bf16[2,2,288,1024]{3,2,1,0:T(8,128)(2,1)} %get-tuple-element.549), channel_id=1, source_target_pairs={{0,1},{1,0},{2,3},{3,2},{4,5},{5,4},{6,7},{7,6},{8,9},{9,8},{10,11... | collective-permute-start | bytes 7077896 | tf_op jit(solution)/shard_map/ppermute | solution.py:966
  381.6 17.3 %collective-permute-start.57 = (bf16[288,1024]{1,0:T(8,128)(2,1)}, bf16[288,1024]{1,0:T(8,128)(2,1)S(1)}, u32[]{:S(2)}, u32[]{:S(2)}) collective-permute-start(bf16[288,1024]{1,0:T(8,128)(2,1)} %fusion.5), channel_id=1, source_target_pairs={{4,0},{5,1},{6,2},{7,3},{8,4},{9,5},{10,6},{11,7},{12,8},{13,9},{1... | collective-permute-start | bytes 1769480 | tf_op jit(solution)/shard_map/ppermute | solution.py:1029
  400.7 29.0 %collective-permute-start.59 = (bf16[2,2,288,1024]{3,2,1,0:T(8,128)(2,1)}, bf16[2,2,288,1024]{3,2,1,0:T(8,128)(2,1)}, u32[]{:S(2)}, u32[]{:S(2)}) collective-permute-start(bf16[2,2,288,1024]{3,2,1,0:T(8,128)(2,1)} %get-tuple-element.566), channel_id=1, source_target_pairs={{0,1},{1,0},{2,3},{3,2},{4,5},{5,4},{6,7},{7,6},{8,9},{9,8},{10,11... | collective-permute-start | bytes 7077896 | tf_op jit(solution)/shard_map/ppermute | solution.py:966
  406.3 18.9 %collective-permute-start.61 = (bf16[288,1024]{1,0:T(8,128)(2,1)}, bf16[288,1024]{1,0:T(8,128)(2,1)}, u32[]{:S(2)}, u32[]{:S(2)}) collective-permute-start(bf16[288,1024]{1,0:T(8,128)(2,1)} %fusion.3), channel_id=1, source_target_pairs={{4,0},{5,1},{6,2},{7,3},{8,4},{9,5},{10,6},{11,7},{12,8},{13,9},{1... | collective-permute-start | bytes 1769480 | tf_op jit(solution)/shard_map/ppermute | solution.py:1029
  406.9 22.9 %collective-permute-start.62 = (bf16[384,1024]{1,0:T(8,128)(2,1)}, bf16[384,1024]{1,0:T(8,128)(2,1)}, u32[]{:S(2)}, u32[]{:S(2)}) collective-permute-start(bf16[384,1024]{1,0:T(8,128)(2,1)} %get-tuple-element.569), channel_id=1, source_target_pairs={{0,16},{16,0},{1,17},{17,1},{2,18},{18,2},{3,19},{19,3},{4,20},{20... | collective-permute-start | bytes 2359304 | tf_op jit(solution)/shard_map/ppermute | solution.py:1032
  408.4 45.5 %all-to-all-start.3 = ((bf16[32,32,256]{2,1,0:T(8,128)(2,1)}), bf16[32,32,256]{2,1,0:T(8,128)(2,1)}, u32[]{:S(2)}, u32[]{:S(2)}) async-start(bf16[32,32,256]{2,1,0:T(8,128)(2,1)} %bitcast.165), calls=%async_computation.3 | async-start | bytes 1048576 | tf_op jit(solution)/shard_map/all_to_all | solution.py:1155
  448.3 20.3 %collective-permute-start.66 = (bf16[288,1024]{1,0:T(8,128)(2,1)}, bf16[288,1024]{1,0:T(8,128)(2,1)}, u32[]{:S(2)}, u32[]{:S(2)}) collective-permute-start(bf16[288,1024]{1,0:T(8,128)(2,1)} %add_convert_fusion.22), channel_id=1, source_target_pairs={{4,0},{5,1},{6,2},{7,3},{8,4},{9,5},{10,6},{11,7},{12,8},{13,9},{1... | collective-permute-start | bytes 1769480 | tf_op jit(solution)/shard_map/ppermute | solution.py:1029
  453.9 33.7 %all-to-all-start.4 = ((bf16[8,32,1152]{2,1,0:T(8,128)(2,1)}), bf16[8,32,1152]{2,1,0:T(8,128)(2,1)S(1)}, u32[]{:S(2)}, u32[]{:S(2)}) async-start(bf16[8,32,1152]{2,1,0:T(8,128)(2,1)} %add_convert_fusion.18), calls=%async_computation.4 | async-start | bytes 1179648 | tf_op jit(solution)/shard_map/all_to_all | solution.py:1151
  (101 other events, 1080.7 us)
Sparse Core Ops, SparseCore 0:
  63.2 92.8 all-gather.2
where the time goes:
time: 509 us; the launch traced here: 500 us
  Pallas kernels  150 us (29%)
  waiting for transfers between devices  140 us (28%)
  starting transfers between devices  103 us (20%)
  other arithmetic  63.8 us (13%)
  local copies, waits for them, and re-layouts  27.6 us (5%)
  between operations  15.6 us (3%)
    ppermute x54, waiting for transfers between devices, move(): lax.ppermute(x, 'ep', (send_to if sender else fetch_from)(ep, **offset))  73.6 us
    ppermute x54, starting transfers between devices, move(): lax.ppermute(x, 'ep', (send_to if sender else fetch_from)(ep, **offset))  49.2 us
    pallas_call x4, Pallas kernels, experts(): pl.pallas_call(functools.partial(expert_kernel, place, cap, zs, dz, first...  48.9 us
    convert_element_type x25, other arithmetic, add_low(): return total.astype(bf16)  34.5 us
    all_to_all x1, waiting for transfers between devices, body(): recv = lax.all_to_all(made, 'ep', split_axis=0, concat_axis=0, tiled=True)  24.2 us
    ppermute x9, waiting for transfers between devices, hop(): return lax.ppermute(value, 'ep', fetch_from(ep, dz=1))  22.4 us
    pallas_call x4, Pallas kernels, project(): pl.pallas_call(functools.partial(project_kernel, place, carried is not No...  21.7 us
    ppermute x4, waiting for transfers between devices, swap(): return [lax.ppermute(piece, 'dp', ring) for ring in rings]  17.7 us
  transfers between devices with their start and end apart: 75, of which 30 were waited for; matrix products, arithmetic and copies ran while one was open for 17% of the time, Pallas kernels for 28%

commit v1 on v0

--- a/solution.py
+++ b/solution.py
@@ -931,23 +931,28 @@
 
     positions = me * span + jnp.arange(span, dtype=jnp.int32)
     is_valid = positions[None, :] < lengths[:, None]
-    expert_range = jnp.arange(LANES, dtype=jnp.int32)
-    hit = expert_ids[..., None] == expert_range
-    chosen = jnp.any(hit, axis=2).reshape(rows, LANES).astype(f32)
-    live = jnp.any(hit & (pair_keep[..., None] > 0), axis=2) & is_valid[..., None]
-    live = live.reshape(rows, LANES).astype(bf16)
-    earlier = jnp.arange(rows)[:, None] > jnp.arange(rows)[None, :]
-    slot = jnp.dot(earlier.astype(bf16), live, preferred_element_type=f32)
-    code = jnp.where((slot < capacity) & (live > 0), slot + 1.0, -chosen)
-    code_rows = -(-expert_count // 16) * 16
-    lines = jnp.pad(code[:, 0:code_rows].T.astype(bf16), ((0, 0), (0, width - rows)))
-    lifted = jnp.concatenate([out_grad, lines])
-
-    rates = theta_base ** (-2.0 * jnp.arange(HD // 2, dtype=f32) / HD)
-    angle = jnp.arange(total, dtype=jnp.int32).astype(f32)[:, None] * rates[None, :]
-    cos = jnp.tile(jnp.cos(angle), (1, 4))
-    sin = jnp.sin(angle)
-    sin = jnp.concatenate([-sin, sin, -sin, sin], axis=1)
+
+    def prepare(earlier_step):
+        expert_range = jnp.arange(LANES, dtype=jnp.int32)
+        hit = phase(expert_ids, earlier_step)[0][..., None] == expert_range
+        chosen = jnp.any(hit, axis=2).reshape(rows, LANES).astype(f32)
+        live = jnp.any(hit & (pair_keep[..., None] > 0), axis=2) & is_valid[..., None]
+        live = live.reshape(rows, LANES).astype(bf16)
+        earlier = jnp.arange(rows)[:, None] > jnp.arange(rows)[None, :]
+        slot = jnp.dot(earlier.astype(bf16), live, preferred_element_type=f32)
+        code = jnp.where((slot < capacity) & (live > 0), slot + 1.0, -chosen)
+        code_rows = -(-expert_count // 16) * 16
+        lines = jnp.pad(code[:, 0:code_rows].T.astype(bf16), ((0, 0), (0, width - rows)))
+        lifted = jnp.concatenate([out_grad, lines])
+
+        rates = theta_base ** (-2.0 * jnp.arange(HD // 2, dtype=f32) / HD)
+        rates = phase(rates, earlier_step)[0]
+        angle = jnp.arange(total, dtype=jnp.int32).astype(f32)[:, None] * rates[None, :]
+        cos = jnp.tile(jnp.cos(angle), (1, 4))
+        sin = jnp.sin(angle)
+        sin = jnp.concatenate([-sin, sin, -sin, sin], axis=1)
+        return code, lifted, cos, sin
+
     core = me % 2
     col = (me // 2) % ys
     plane = me // place
@@ -997,7 +1002,9 @@
             near[t] = [columns[t]] + y_new
         if on_core:
             far[t - 1] = c_new
-        if t == 2:
+        if t == 0:
+            code, lifted, cos, sin = prepare(columns[-1])
+        if t == len(order) - 2:
             upstream = lax.all_gather(phase(lifted, columns[-1])[0], "ep", axis=0)
     wo_new = [
         lax.ppermute(wo_part[0], "dp", [((i + k) % dp, i) for i in range(dp)]) for k in range(1, dp)

time: 509 us -> 505 us (level)
  transfers between devices with their start and end apart: 75 -> 75, of which waited for: 30 -> 33; matrix products, arithmetic and copies ran while one was open for 17% -> 16% of each run, Pallas kernels for 28% -> 29%
where the time goes in v1:
time: 505 us; the launch traced here: 497 us
  Pallas kernels  150 us (30%)
  waiting for transfers between devices  144 us (29%)
  starting transfers between devices  98 us (19%)
  other arithmetic  63.8 us (13%)
  local copies, waits for them, and re-layouts  25 us (5%)
  between operations  15.6 us (3%)
    ppermute x54, waiting for transfers between devices, move(): lax.ppermute(x, 'ep', (send_to if sender else fetch_from)(ep, **offset))  76.3 us
    ppermute x54, starting transfers between devices, move(): lax.ppermute(x, 'ep', (send_to if sender else fetch_from)(ep, **offset))  49.2 us
    pallas_call x4, Pallas kernels, experts(): pl.pallas_call(functools.partial(expert_kernel, place, cap, zs, dz, first...  48.9 us
    convert_element_type x25, other arithmetic, add_low(): return total.astype(bf16)  34.5 us
    all_to_all x1, waiting for transfers between devices, body(): recv = lax.all_to_all(made, 'ep', split_axis=0, concat_axis=0, tiled=True)  24.4 us
    ppermute x9, waiting for transfers between devices, hop(): return lax.ppermute(value, 'ep', fetch_from(ep, dz=1))  23.8 us
    pallas_call x4, Pallas kernels, project(): pl.pallas_call(functools.partial(project_kernel, place, carried is not No...  21.7 us
    pallas_call x1, Pallas kernels, back(): pl.pallas_call(functools.partial(back_kernel, replicas), grid=(seqs,), ou...  17.6 us
  transfers between devices with their start and end apart: 75, of which 33 were waited for; matrix products, arithmetic and copies ran while one was open for 16% of the time, Pallas kernels for 29%

profile of v1, /device:TPU:8, one launch (start us, length us, event | category | flops | bytes accessed | tf_op | source)
XLA Modules:
  0.0 496.6 jit_solution(8897992331337671895)
XLA Ops:
  14.1 5.9 %all-to-all-start = ((bf16[32,32,256]{2,1,0:T(8,128)(2,1)}), bf16[32,32,256]{2,1,0:T(8,128)(2,1)S(1)}, u32[]{:S(2)}, u32[]{:S(2)}) async-start(bf16[32,32,256]{2,1,0:T(8,128)(2,1)} %bitcast.9), calls=%async_computation | async-start | bytes 1048576 | tf_op jit(solution)/shard_map/all_to_all | solution.py:923
  22.9 7.0 %collective-permute-start.2 = (bf16[288,1024]{1,0:T(8,128)(2,1)}, bf16[288,1024]{1,0:T(8,128)(2,1)}, u32[]{:S(2)}, u32[]{:S(2)}) collective-permute-start(bf16[288,1024]{1,0:T(8,128)(2,1)} %collective-permute-done.refs_0_), channel_id=1, source_target_pairs={{4,0},{5,1},{6,2},{7,3},{8,4},{9,5},{10,6},{11,7},{12,8},{13,9},{1... | collective-permute-start | bytes 1769480 | tf_op jit(solution)/shard_map/ppermute | solution.py:971
  40.6 6.0 %collective-permute-done.2.refs_0_ = bf16[288,1024]{1,0:T(8,128)(2,1)} collective-permute-done((bf16[288,1024]{1,0:T(8,128)(2,1)}, bf16[288,1024]{1,0:T(8,128)(2,1)}, u32[]{:S(2)}, u32[]{:S(2)}) %collective-permute-start.2) | collective-permute-done | bytes 589856 | tf_op jit(solution)/shard_map/ppermute | solution.py:971
  50.9 5.5 %project_in.4 = (bf16[4,4,288,1024]{3,2,1,0:T(8,128)(2,1)}, bf16[4,4,288,256]{3,2,1,0:T(8,128)(2,1)}) custom-call(s32[5]{0:T(128)} %pad_add_fusion.meta, bf16[288,1024]{1,0:T(8,128)(2,1)} %bitcast.refs_0_.hid_ref, bf16[288,1024]{1,0:T(8,128)(2,1)} %collective-permute-done.1.refs_1_, bf16[288,1024]{1,0:T(8,128)(2,1)} %collective-permute-done.4.refs_2_, ...), custom_call_target="tpu_custom_call" | custom-call | flops 603979776 | bytes 4718592 | tf_op jit(solution)/shard_map/project_in/pallas_call | solution.py:119
  56.3 5.4 %collective-permute-done.6.refs_0_ = bf16[288,1024]{1,0:T(8,128)(2,1)S(1)} collective-permute-done((bf16[288,1024]{1,0:T(8,128)(2,1)}, bf16[288,1024]{1,0:T(8,128)(2,1)S(1)}, u32[]{:S(2)}, u32[]{:S(2)}) %collective-permute-start.6) | collective-permute-done | bytes 589856 | tf_op jit(solution)/shard_map/ppermute | solution.py:971
  70.6 5.6 %project_in.5 = (bf16[4,4,288,1024]{3,2,1,0:T(8,128)(2,1)}, bf16[4,4,288,256]{3,2,1,0:T(8,128)(2,1)}) custom-call(s32[5]{0:T(128)} %pad_add_fusion.meta, bf16[288,1024]{1,0:T(8,128)(2,1)} %collective-permute-done.refs_0_, bf16[288,1024]{1,0:T(8,128)(2,1)} %collective-permute-done.3.refs_1_, ...), custom_call_target="tpu_custom_call", output_to_operand_aliasing={{0}: (9, {}), {1}: (10, {})} | custom-call | flops 603979776 | bytes 4718592 | tf_op jit(solution)/shard_map/project_in/pallas_call | solution.py:119
  83.1 5.4 %project_in.6 = (bf16[4,4,288,1024]{3,2,1,0:T(8,128)(2,1)}, bf16[4,4,288,256]{3,2,1,0:T(8,128)(2,1)}) custom-call(s32[5]{0:T(128)} %pad_add_fusion.meta, bf16[288,1024]{1,0:T(8,128)(2,1)} %collective-permute-done.2.refs_0_, bf16[288,1024]{1,0:T(8,128)(2,1)} %copy-done.19, ...), custom_call_target="tpu_custom_call", output_to_operand_aliasing={{0}: (9, {}), {1}: (10, {})} | custom-call | flops 603979776 | bytes 4718592 | tf_op jit(solution)/shard_map/project_in/pallas_call | solution.py:119
  90.7 5.3 %project_in.7 = (bf16[4,4,288,1024]{3,2,1,0:T(8,128)(2,1)}, bf16[4,4,288,256]{3,2,1,0:T(8,128)(2,1)}) custom-call(s32[5]{0:T(128)} %pad_add_fusion.meta, bf16[288,1024]{1,0:T(8,128)(2,1)} %copy-done.18, bf16[288,1024]{1,0:T(8,128)(2,1)} %copy-done.20, bf16[288,1024]{1,0:T(8,128)(2,1)} %copy-done.27, ...), custom_call_target="tpu_custom_call", output_to_operand_aliasing={{0}: (9, {}), {1}: (10, {})} | custom-call | flops 603979776 | bytes 4718592 | tf_op jit(solution)/shard_map/project_in/pallas_call | solution.py:119
  98.3 11.2 %attend_forward.1 = (bf16[16,144,128]{2,1,0:T(8,128)(2,1)}, bf16[3,1536,128]{2,1,0:T(8,128)(2,1)}, bf16[3,1536,128]{2,1,0:T(8,128)(2,1)}, bf16[3,128,1536]{2,1,0:T(8,128)(2,1)}, f32[3,72,1536]{2,1,0:T(8,128)}) custom-call(s32[12]{0:T(128)} %concatenate.34.meta, bf16[4,4,288,256]{3,2,1,0:T(8,128)(2,1)} %get-tuple-element.361.qkv_ref), custom_call_target="tpu_custom_call" | custom-call | flops 3623878656 | bytes 4718592 | tf_op jit(solution)/shard_map/attend_forward/pallas_call | solution.py:220
  111.6 7.1 %all-to-all-start.1 = ((bf16[16,144,128]{2,1,0:T(8,128)(2,1)}), bf16[16,144,128]{2,1,0:T(8,128)(2,1)}, u32[]{:S(2)}, u32[]{:S(2)}) async-start(bf16[16,144,128]{2,1,0:T(8,128)(2,1)} %get-tuple-element.364), calls=%async_computation.1 | async-start | bytes 1179648 | tf_op jit(solution)/shard_map/all_to_all | solution.py:1015
  123.1 24.4 %all-to-all-done.1.recv_ref = bf16[16,144,128]{2,1,0:T(8,128)(2,1)} async-done(((bf16[16,144,128]{2,1,0:T(8,128)(2,1)}), bf16[16,144,128]{2,1,0:T(8,128)(2,1)}, u32[]{:S(2)}, u32[]{:S(2)}) %all-to-all-start.1) | async-done | bytes 589856 | tf_op jit(solution)/shard_map/all_to_all | solution.py:1015
  147.5 4.5 project_out.1
  155.8 12.8 %collective-permute-done.21.refs_0_ = bf16[288,1024]{1,0:T(8,128)(2,1)S(1)} collective-permute-done((bf16[288,1024]{1,0:T(8,128)(2,1)}, bf16[288,1024]{1,0:T(8,128)(2,1)S(1)}, u32[]{:S(2)}, u32[]{:S(2)}) %collective-permute-start.21) | collective-permute-done | bytes 589856 | tf_op jit(solution)/shard_map/ppermute | solution.py:971
  173.6 10.9 %collective-permute-done.23.refs_0_ = bf16[288,1024]{1,0:T(8,128)(2,1)S(1)} collective-permute-done((bf16[288,1024]{1,0:T(8,128)(2,1)S(1)}, bf16[288,1024]{1,0:T(8,128)(2,1)S(1)}, u32[]{:S(2)}, u32[]{:S(2)}) %collective-permute-start.23) | collective-permute-done | bytes 589856 | tf_op jit(solution)/shard_map/ppermute | solution.py:971
  192.0 12.1 %experts.4 = (bf16[2,304,1024]{2,1,0:T(8,128)(2,1)}, bf16[2,304,1024]{2,1,0:T(8,128)(2,1)}, bf16[4,2,288,1024]{3,2,1,0:T(8,128)(2,1)}, bf16[4,2,288,1024]{3,2,1,...) custom-call(s32[6]{0:T(128)} %pad_add_fusion.2.meta, ...), custom_call_target="tpu_custom_call" | custom-call | flops 4831838208 | bytes 7077888 | tf_op jit(solution)/shard_map/experts/pallas_call | solution.py:456
  205.2 12.4 %experts.5 = (bf16[2,304,1024]{2,1,0:T(8,128)(2,1)}, bf16[2,304,1024]{2,1,0:T(8,128)(2,1)}, bf16[4,2,288,1024]{3,2,1,0:T(8,128)(2,1)}, bf16[4,2,288,1024]{3,2,1,...) custom-call(s32[6]{0:T(128)} %pad_add_fusion.2.meta, ...), custom_call_target="tpu_custom_call", output_to_operand_aliasing={{2}: (9, {}), {3}: (10, {}), {4}: (11, {}), {5}: (12, {}), ... | custom-call | flops 4831838208 | bytes 7077888 | tf_op jit(solution)/shard_map/experts/pallas_call | solution.py:456
  222.5 12.1 %experts.6 = (bf16[2,304,1024]{2,1,0:T(8,128)(2,1)}, bf16[2,304,1024]{2,1,0:T(8,128)(2,1)}, bf16[4,2,288,1024]{3,2,1,0:T(8,128)(2,1)}, bf16[4,2,288,1024]{3,2,1,...) custom-call(s32[6]{0:T(128)} %pad_add_fusion.2.meta, ...), custom_call_target="tpu_custom_call", output_to_operand_aliasing={{2}: (9, {}), {3}: (10, {}), {4}: (11, {}), {5}: (12, {}), ... | custom-call | flops 4831838208 | bytes 7077888 | tf_op jit(solution)/shard_map/experts/pallas_call | solution.py:456
  240.6 12.3 %experts.7 = (bf16[2,304,1024]{2,1,0:T(8,128)(2,1)}, bf16[2,304,1024]{2,1,0:T(8,128)(2,1)}, bf16[4,2,288,1024]{3,2,1,0:T(8,128)(2,1)}, bf16[4,2,288,1024]{3,2,1,...) custom-call(s32[6]{0:T(128)} %pad_add_fusion.2.meta, ...), custom_call_target="tpu_custom_call", output_to_operand_aliasing={{2}: (9, {}), {3}: (10, {}), {4}: (11, {}), {5}: (12, {}), ... | custom-call | flops 4831838208 | bytes 7077888 | tf_op jit(solution)/shard_map/experts/pallas_call | solution.py:456
  262.3 15.3 %expert_grads.1 = (bf16[384,1024]{1,0:T(8,128)(2,1)}, bf16[384,1024]{1,0:T(8,128)(2,1)}, bf16[384,1024]{1,0:T(8,128)(2,1)}, bf16[384,1024]{1,0:T(8,128)(2,1)}) custom-call(bf16[4,576,1024]{2,1,0:T(8,128)(2,1)} %get-tuple-element.475.x_ref, bf16[4,576,1024]{2,1,0:T(8,128)(2,1)} %get-tuple-element.478.both_ref, ...), custom_call_target="tpu_custom_call" | custom-call | flops 7247757312 | bytes 18874368 | tf_op jit(solution)/shard_map/expert_grads/pallas_call | solution.py:729
  300.9 11.0 %collective-permute-done.48 = bf16[1,288,1024]{2,1,0:T(8,128)(2,1)S(1)} collective-permute-done((bf16[1,288,1024]{2,1,0:T(8,128)(2,1)S(1)}, bf16[1,288,1024]{2,1,0:T(8,128)(2,1)S(1)}, u32[]{:S(2)}, u32[]{:S(2)}) %collective-permute-start.48) | collective-permute-done | bytes 589856 | tf_op jit(solution)/shard_map/ppermute | solution.py:971
  315.6 6.1 %turn_back.1 = (f32[288,1024]{1,0:T(8,128)}, bf16[288,1024]{1,0:T(8,128)(2,1)}, bf16[16,144,128]{2,1,0:T(8,128)(2,1)}, f32[288,128]{1,0:T(8,128)}, f32[1,1024]{1,0:T(1,128)}) custom-call(s32[4]{0:T(128)} %pad_add_fusion.1.meta, bf16[304,1024]{1,0:T(8,128)(2,1)} %add_convert_fusion.13.refs_0_, bf16[304,1024]{1,0:T(8,128)(2,1)} %copy-done.17, ...), custom_call_target="tpu_custom_call" | custom-call | flops 1207959552 | bytes 4194304 | tf_op jit(solution)/shard_map/turn_back/pallas_call | solution.py:562
  321.8 6.5 %all-to-all-start.2 = ((bf16[16,144,128]{2,1,0:T(8,128)(2,1)}), bf16[16,144,128]{2,1,0:T(8,128)(2,1)}, u32[]{:S(2)}, u32[]{:S(2)}) async-start(bf16[16,144,128]{2,1,0:T(8,128)(2,1)} %get-tuple-element.514), calls=%async_computation.2 | async-start | bytes 1179648 | tf_op jit(solution)/shard_map/all_to_all | solution.py:1111
  329.2 4.6 late_grads.1
  337.6 10.5 %collective-permute-done.51 = bf16[384,1024]{1,0:T(8,128)(2,1)} collective-permute-done((bf16[384,1024]{1,0:T(8,128)(2,1)}, bf16[384,1024]{1,0:T(8,128)(2,1)}, u32[]{:S(2)}, u32[]{:S(2)}) %collective-permute-start.51) | collective-permute-done | bytes 786464 | tf_op jit(solution)/shard_map/ppermute | solution.py:1039
  353.1 17.6 %attend_backward.1.dqkv_ref = bf16[4,4,288,256]{3,2,1,0:T(8,128)(2,1)} custom-call(s32[12]{0:T(128)} %concatenate.34.meta, bf16[16,144,128]{2,1,0:T(8,128)(2,1)} %all-to-all-done.2.grad_ref, bf16[3,1536,128]{2,1,0:T(8,128)(2,1)} %get-tuple-element.532.qk_ref, bf16[3,1536,128]{2,1,0:T(8,128)(2,1)} %get-tuple-element.533.v_ref, ...), custom_call_target="tpu_custom_call" | custom-call | flops 9059696640 | bytes 7077888 | tf_op jit(solution)/shard_map/attend_backward/pallas_call | solution.py:671
  370.8 4.9 spread.2
  386.9 7.8 %head_grads.1 = bf16[1024,256]{1,0:T(8,128)(2,1)} custom-call(bf16[4,4,288,256]{3,2,1,0:T(8,128)(2,1)} %attend_backward.1.dqkv_ref, bf16[4,4,288,1024]{3,2,1,0:T(8,128)(2,1)} %get-tuple-element.559.normed_ref), custom_call_target="tpu_custom_call" | custom-call | flops 2415919104 | bytes 9437184 | tf_op jit(solution)/shard_map/head_grads/pallas_call | solution.py:789
  404.4 5.2 %all-to-all-start.3 = ((bf16[32,32,256]{2,1,0:T(8,128)(2,1)}), bf16[32,32,256]{2,1,0:T(8,128)(2,1)}, u32[]{:S(2)}, u32[]{:S(2)}) async-start(bf16[32,32,256]{2,1,0:T(8,128)(2,1)} %bitcast.159), calls=%async_computation.3 | async-start | bytes 1048576 | tf_op jit(solution)/shard_map/all_to_all | solution.py:1162
  421.6 4.6 collective-permute-done.62
  450.3 5.5 %all-to-all-start.4 = ((bf16[8,32,1152]{2,1,0:T(8,128)(2,1)}), bf16[8,32,1152]{2,1,0:T(8,128)(2,1)S(1)}, u32[]{:S(2)}, u32[]{:S(2)}) async-start(bf16[8,32,1152]{2,1,0:T(8,128)(2,1)} %add_convert_fusion.18), calls=%async_computation.4 | async-start | bytes 1179648 | tf_op jit(solution)/shard_map/all_to_all | solution.py:1158
  457.3 7.7 %collective-permute-done.66 = bf16[288,1024]{1,0:T(8,128)(2,1)} collective-permute-done((bf16[288,1024]{1,0:T(8,128)(2,1)}, bf16[288,1024]{1,0:T(8,128)(2,1)}, u32[]{:S(2)}, u32[]{:S(2)}) %collective-permute-start.66) | collective-permute-done | bytes 589856 | tf_op jit(solution)/shard_map/ppermute | solution.py:1036
  476.1 6.7 %collective-permute-done.68.refs_4_ = bf16[288,1024]{1,0:T(8,128)(2,1)S(1)} collective-permute-done((bf16[288,1024]{1,0:T(8,128)(2,1)}, bf16[288,1024]{1,0:T(8,128)(2,1)S(1)}, u32[]{:S(2)}, u32[]{:S(2)}) %collective-permute-start.68) | collective-permute-done | bytes 589856 | tf_op jit(solution)/shard_map/ppermute | solution.py:1036
  (364 shorter events, 201.5 us)
Async XLA Ops:
  14.1 34.6 %all-to-all-start = ((bf16[32,32,256]{2,1,0:T(8,128)(2,1)}), bf16[32,32,256]{2,1,0:T(8,128)(2,1)S(1)}, u32[]{:S(2)}, u32[]{:S(2)}) async-start(bf16[32,32,256]{2,1,0:T(8,128)(2,1)} %bitcast.9), calls=%async_computation | async-start | bytes 1048576 | tf_op jit(solution)/shard_map/all_to_all | solution.py:923
  20.0 172.0 %all-gather.3.cloned.1.call-start = ((), (), s32[]{:S(2)}) async-start(), calls=%async_computation.5 | async-start | bytes 10584064 | tf_op jit(solution)/shard_map/all_gather | solution.py:1008
  22.9 23.7 %collective-permute-start.2 = (bf16[288,1024]{1,0:T(8,128)(2,1)}, bf16[288,1024]{1,0:T(8,128)(2,1)}, u32[]{:S(2)}, u32[]{:S(2)}) collective-permute-start(bf16[288,1024]{1,0:T(8,128)(2,1)} %collective-permute-done.refs_0_), channel_id=1, source_target_pairs={{4,0},{5,1},{6,2},{7,3},{8,4},{9,5},{10,6},{11,7},{12,8},{13,9},{1... | collective-permute-start | bytes 1769480 | tf_op jit(solution)/shard_map/ppermute | solution.py:971
  29.9 16.7 %collective-permute-start.3 = (bf16[288,1024]{1,0:T(8,128)(2,1)}, bf16[288,1024]{1,0:T(8,128)(2,1)}, u32[]{:S(2)}, u32[]{:S(2)}) collective-permute-start(bf16[288,1024]{1,0:T(8,128)(2,1)} %collective-permute-done.refs_0_), channel_id=1, source_target_pairs={{2,0},{3,1},{0,2},{1,3},{6,4},{7,5},{4,6},{5,7},{10,8},{11,9},{8,1... | collective-permute-start | bytes 1769480 | tf_op jit(solution)/shard_map/ppermute | solution.py:971
  61.9 18.0 %collective-permute-start.10 = (bf16[288,1024]{1,0:T(8,128)(2,1)S(1)}, bf16[288,1024]{1,0:T(8,128)(2,1)S(1)}, u32[]{:S(2)}, u32[]{:S(2)}) collective-permute-start(bf16[288,1024]{1,0:T(8,128)(2,1)S(1)} %collective-permute-done.6.refs_0_), channel_id=1, source_target_pairs={{2,0},{3,1},{0,2},{1,3},{6,4},{7,5},{4,6},{5,7},{10,8},{11,9},{8,1... | collective-permute-start | bytes 1769480 | tf_op jit(solution)/shard_map/ppermute | solution.py:971
  111.6 35.9 %all-to-all-start.1 = ((bf16[16,144,128]{2,1,0:T(8,128)(2,1)}), bf16[16,144,128]{2,1,0:T(8,128)(2,1)}, u32[]{:S(2)}, u32[]{:S(2)}) async-start(bf16[16,144,128]{2,1,0:T(8,128)(2,1)} %get-tuple-element.364), calls=%async_computation.1 | async-start | bytes 1179648 | tf_op jit(solution)/shard_map/all_to_all | solution.py:1015
  152.0 16.7 %collective-permute-start.21 = (bf16[288,1024]{1,0:T(8,128)(2,1)}, bf16[288,1024]{1,0:T(8,128)(2,1)S(1)}, u32[]{:S(2)}, u32[]{:S(2)}) collective-permute-start(bf16[288,1024]{1,0:T(8,128)(2,1)} %get-tuple-element.523.refs_0_.pay_ref), channel_id=1, source_target_pairs={{4,0},{5,1},{6,2},{7,3},{8,4},{9,5},{10,6},{11,7},{12,8},{13,9},{1... | collective-permute-start | bytes 1769480 | tf_op jit(solution)/shard_map/ppermute | solution.py:971
  152.0 17.7 %collective-permute-start.22 = (bf16[288,1024]{1,0:T(8,128)(2,1)}, bf16[288,1024]{1,0:T(8,128)(2,1)S(1)}, u32[]{:S(2)}, u32[]{:S(2)}) collective-permute-start(bf16[288,1024]{1,0:T(8,128)(2,1)} %get-tuple-element.523.refs_0_.pay_ref), channel_id=1, source_target_pairs={{2,0},{3,1},{0,2},{1,3},{6,4},{7,5},{4,6},{5,7},{10,8},{11,9},{8,1... | collective-permute-start | bytes 1769480 | tf_op jit(solution)/shard_map/ppermute | solution.py:971
  186.8 17.3 %collective-permute-start.27 = (bf16[288,1024]{1,0:T(8,128)(2,1)S(1)}, bf16[288,1024]{1,0:T(8,128)(2,1)S(1)}, u32[]{:S(2)}, u32[]{:S(2)}) collective-permute-start(bf16[288,1024]{1,0:T(8,128)(2,1)S(1)} %collective-permute-done.23.refs_0_), channel_id=1, source_target_pairs={{4,0},{5,1},{6,2},{7,3},{8,4},{9,5},{10,6},{11,7},{12,8},{13,9},{1... | collective-permute-start | bytes 1769480 | tf_op jit(solution)/shard_map/ppermute | solution.py:971
  221.1 17.0 %collective-permute-start.37 = (bf16[2,304,1024]{2,1,0:T(8,128)(2,1)}, bf16[2,304,1024]{2,1,0:T(8,128)(2,1)S(1)}, u32[]{:S(2)}, u32[]{:S(2)}) collective-permute-start(bf16[2,304,1024]{2,1,0:T(8,128)(2,1)} %get-tuple-element.424), channel_id=1, source_target_pairs={{0,1},{1,0},{2,3},{3,2},{4,5},{5,4},{6,7},{7,6},{8,9},{9,8},{10,11... | collective-permute-start | bytes 3735560 | tf_op jit(solution)/shard_map/ppermute | solution.py:971
  221.7 16.5 %collective-permute-start.38 = (bf16[304,1024]{1,0:T(8,128)(2,1)S(1)}, bf16[304,1024]{1,0:T(8,128)(2,1)S(1)}, u32[]{:S(2)}, u32[]{:S(2)}) collective-permute-start(bf16[304,1024]{1,0:T(8,128)(2,1)S(1)} %get-tuple-element.737), channel_id=1, source_target_pairs={{0,2},{1,3},{2,0},{3,1},{4,6},{5,7},{6,4},{7,5},{8,10},{9,11},{10,... | collective-permute-start | bytes 1867784 | tf_op jit(solution)/shard_map/ppermute | solution.py:971
  238.2 17.5 %collective-permute-start.39 = (bf16[2,304,1024]{2,1,0:T(8,128)(2,1)}, bf16[2,304,1024]{2,1,0:T(8,128)(2,1)S(1)}, u32[]{:S(2)}, u32[]{:S(2)}) collective-permute-start(bf16[2,304,1024]{2,1,0:T(8,128)(2,1)} %get-tuple-element.447), channel_id=1, source_target_pairs={{0,1},{1,0},{2,3},{3,2},{4,5},{5,4},{6,7},{7,6},{8,9},{9,8},{10,11... | collective-permute-start | bytes 3735560 | tf_op jit(solution)/shard_map/ppermute | solution.py:971
  255.7 21.9 %collective-permute-start.44 = (bf16[4,2,288,1024]{3,2,1,0:T(8,128)(2,1)}, bf16[4,2,288,1024]{3,2,1,0:T(8,128)(2,1)}, u32[]{:S(2)}, u32[]{:S(2)}) collective-permute-start(bf16[4,2,288,1024]{3,2,1,0:T(8,128)(2,1)} %get-tuple-element.474), channel_id=1, source_target_pairs={{0,1},{1,0},{2,3},{3,2},{4,5},{5,4},{6,7},{7,6},{8,9},{9,8},{10,11... | collective-permute-start | bytes 14155784 | tf_op jit(solution)/shard_map/ppermute | solution.py:971
  255.7 21.9 %collective-permute-start.41 = (bf16[2,304,1024]{2,1,0:T(8,128)(2,1)}, bf16[2,304,1024]{2,1,0:T(8,128)(2,1)S(1)}, u32[]{:S(2)}, u32[]{:S(2)}) collective-permute-start(bf16[2,304,1024]{2,1,0:T(8,128)(2,1)} %get-tuple-element.468), channel_id=1, source_target_pairs={{0,1},{1,0},{2,3},{3,2},{4,5},{5,4},{6,7},{7,6},{8,9},{9,8},{10,11... | collective-permute-start | bytes 3735560 | tf_op jit(solution)/shard_map/ppermute | solution.py:971
  257.5 20.0 %collective-permute-start.42 = (bf16[304,1024]{1,0:T(8,128)(2,1)}, bf16[304,1024]{1,0:T(8,128)(2,1)}, u32[]{:S(2)}, u32[]{:S(2)}) collective-permute-start(bf16[304,1024]{1,0:T(8,128)(2,1)} %get-tuple-element.733), channel_id=1, source_target_pairs={{0,2},{1,3},{2,0},{3,1},{4,6},{5,7},{6,4},{7,5},{8,10},{9,11},{10,... | collective-permute-start | bytes 1867784 | tf_op jit(solution)/shard_map/ppermute | solution.py:971
  260.1 17.4 %collective-permute-start.43 = (bf16[304,1024]{1,0:T(8,128)(2,1)}, bf16[304,1024]{1,0:T(8,128)(2,1)}, u32[]{:S(2)}, u32[]{:S(2)}) collective-permute-start(bf16[304,1024]{1,0:T(8,128)(2,1)} %add_convert_fusion.10), channel_id=1, source_target_pairs={{4,0},{5,1},{6,2},{7,3},{8,4},{9,5},{10,6},{11,7},{12,8},{13,9},{1... | collective-permute-start | bytes 1867784 | tf_op jit(solution)/shard_map/ppermute | solution.py:1036
  296.7 17.8 %collective-permute-start.49 = (bf16[384,1024]{1,0:T(8,128)(2,1)S(1)}, bf16[384,1024]{1,0:T(8,128)(2,1)S(1)}, u32[]{:S(2)}, u32[]{:S(2)}) collective-permute-start(bf16[384,1024]{1,0:T(8,128)(2,1)S(1)} %copy-done.11), channel_id=1, source_target_pairs={{0,16},{16,0},{1,17},{17,1},{2,18},{18,2},{3,19},{19,3},{4,20},{20... | collective-permute-start | bytes 2359304 | tf_op jit(solution)/shard_map/ppermute | solution.py:1039
  315.3 32.9 %collective-permute-start.50 = (bf16[2,288,1024]{2,1,0:T(8,128)(2,1)}, bf16[2,288,1024]{2,1,0:T(8,128)(2,1)}, u32[]{:S(2)}, u32[]{:S(2)}) collective-permute-start(bf16[2,288,1024]{2,1,0:T(8,128)(2,1)} %add_convert_fusion.2), channel_id=1, source_target_pairs={{0,2},{1,3},{2,0},{3,1},{4,6},{5,7},{6,4},{7,5},{8,10},{9,11},{10,... | collective-permute-start | bytes 3538952 | tf_op jit(solution)/shard_map/ppermute | solution.py:971
  321.8 26.4 %all-to-all-start.2 = ((bf16[16,144,128]{2,1,0:T(8,128)(2,1)}), bf16[16,144,128]{2,1,0:T(8,128)(2,1)}, u32[]{:S(2)}, u32[]{:S(2)}) async-start(bf16[16,144,128]{2,1,0:T(8,128)(2,1)} %get-tuple-element.514), calls=%async_computation.2 | async-start | bytes 1179648 | tf_op jit(solution)/shard_map/all_to_all | solution.py:1111
  328.3 19.9 %collective-permute-start.51 = (bf16[384,1024]{1,0:T(8,128)(2,1)}, bf16[384,1024]{1,0:T(8,128)(2,1)}, u32[]{:S(2)}, u32[]{:S(2)}) collective-permute-start(bf16[384,1024]{1,0:T(8,128)(2,1)} %get-tuple-element.604), channel_id=1, source_target_pairs={{0,16},{16,0},{1,17},{17,1},{2,18},{18,2},{3,19},{19,3},{4,20},{20... | collective-permute-start | bytes 2359304 | tf_op jit(solution)/shard_map/ppermute | solution.py:1039
  348.2 22.6 %collective-permute-start.54 = (bf16[2,8,32,1152]{3,2,1,0:T(8,128)(2,1)}, bf16[2,8,32,1152]{3,2,1,0:T(8,128)(2,1)S(1)}, u32[]{:S(2)}, u32[]{:S(2)}) collective-permute-start(bf16[2,8,32,1152]{3,2,1,0:T(8,128)(2,1)} %get-tuple-element.542), channel_id=1, source_target_pairs={{0,1},{1,0},{2,3},{3,2},{4,5},{5,4},{6,7},{7,6},{8,9},{9,8},{10,11... | collective-permute-start | bytes 3538952 | tf_op jit(solution)/shard_map/ppermute | solution.py:971
  348.2 22.5 %collective-permute-start.52 = (bf16[1,288,1024]{2,1,0:T(8,128)(2,1)}, bf16[1,288,1024]{2,1,0:T(8,128)(2,1)S(1)}, u32[]{:S(2)}, u32[]{:S(2)}) collective-permute-start(bf16[1,288,1024]{2,1,0:T(8,128)(2,1)} %get-tuple-element.539), channel_id=1, source_target_pairs={{0,2},{1,3},{2,0},{3,1},{4,6},{5,7},{6,4},{7,5},{8,10},{9,11},{10,... | collective-permute-start | bytes 1769480 | tf_op jit(solution)/shard_map/ppermute | solution.py:971
  349.7 21.0 %collective-permute-start.53 = (bf16[288,1024]{1,0:T(8,128)(2,1)}, bf16[288,1024]{1,0:T(8,128)(2,1)S(1)}, u32[]{:S(2)}, u32[]{:S(2)}) collective-permute-start(bf16[288,1024]{1,0:T(8,128)(2,1)} %bitcast.57), channel_id=1, source_target_pairs={{4,0},{5,1},{6,2},{7,3},{8,4},{9,5},{10,6},{11,7},{12,8},{13,9},{1... | collective-permute-start | bytes 1769480 | tf_op jit(solution)/shard_map/ppermute | solution.py:1036
  350.5 20.3 %collective-permute-start.55 = (bf16[384,1024]{1,0:T(8,128)(2,1)}, bf16[384,1024]{1,0:T(8,128)(2,1)S(1)}, u32[]{:S(2)}, u32[]{:S(2)}) collective-permute-start(bf16[384,1024]{1,0:T(8,128)(2,1)} %get-tuple-element.606), channel_id=1, source_target_pairs={{0,16},{16,0},{1,17},{17,1},{2,18},{18,2},{3,19},{19,3},{4,20},{20... | collective-permute-start | bytes 2359304 | tf_op jit(solution)/shard_map/ppermute | solution.py:1039
  375.7 21.3 %collective-permute-start.56 = (bf16[2,2,288,1024]{3,2,1,0:T(8,128)(2,1)}, bf16[2,2,288,1024]{3,2,1,0:T(8,128)(2,1)}, u32[]{:S(2)}, u32[]{:S(2)}) collective-permute-start(bf16[2,2,288,1024]{3,2,1,0:T(8,128)(2,1)} %get-tuple-element.553), channel_id=1, source_target_pairs={{0,1},{1,0},{2,3},{3,2},{4,5},{5,4},{6,7},{7,6},{8,9},{9,8},{10,11... | collective-permute-start | bytes 7077896 | tf_op jit(solution)/shard_map/ppermute | solution.py:971
  378.0 16.9 %collective-permute-start.57 = (bf16[288,1024]{1,0:T(8,128)(2,1)}, bf16[288,1024]{1,0:T(8,128)(2,1)S(1)}, u32[]{:S(2)}, u32[]{:S(2)}) collective-permute-start(bf16[288,1024]{1,0:T(8,128)(2,1)} %fusion.5), channel_id=1, source_target_pairs={{4,0},{5,1},{6,2},{7,3},{8,4},{9,5},{10,6},{11,7},{12,8},{13,9},{1... | collective-permute-start | bytes 1769480 | tf_op jit(solution)/shard_map/ppermute | solution.py:1036
  397.1 29.1 %collective-permute-start.59 = (bf16[2,2,288,1024]{3,2,1,0:T(8,128)(2,1)}, bf16[2,2,288,1024]{3,2,1,0:T(8,128)(2,1)}, u32[]{:S(2)}, u32[]{:S(2)}) collective-permute-start(bf16[2,2,288,1024]{3,2,1,0:T(8,128)(2,1)} %get-tuple-element.570), channel_id=1, source_target_pairs={{0,1},{1,0},{2,3},{3,2},{4,5},{5,4},{6,7},{7,6},{8,9},{9,8},{10,11... | collective-permute-start | bytes 7077896 | tf_op jit(solution)/shard_map/ppermute | solution.py:971
  402.7 19.0 %collective-permute-start.61 = (bf16[288,1024]{1,0:T(8,128)(2,1)}, bf16[288,1024]{1,0:T(8,128)(2,1)}, u32[]{:S(2)}, u32[]{:S(2)}) collective-permute-start(bf16[288,1024]{1,0:T(8,128)(2,1)} %fusion.3), channel_id=1, source_target_pairs={{4,0},{5,1},{6,2},{7,3},{8,4},{9,5},{10,6},{11,7},{12,8},{13,9},{1... | collective-permute-start | bytes 1769480 | tf_op jit(solution)/shard_map/ppermute | solution.py:1036
  403.2 23.0 %collective-permute-start.62 = (bf16[384,1024]{1,0:T(8,128)(2,1)}, bf16[384,1024]{1,0:T(8,128)(2,1)}, u32[]{:S(2)}, u32[]{:S(2)}) collective-permute-start(bf16[384,1024]{1,0:T(8,128)(2,1)} %get-tuple-element.573), channel_id=1, source_target_pairs={{0,16},{16,0},{1,17},{17,1},{2,18},{18,2},{3,19},{19,3},{4,20},{20... | collective-permute-start | bytes 2359304 | tf_op jit(solution)/shard_map/ppermute | solution.py:1039
  404.4 45.9 %all-to-all-start.3 = ((bf16[32,32,256]{2,1,0:T(8,128)(2,1)}), bf16[32,32,256]{2,1,0:T(8,128)(2,1)}, u32[]{:S(2)}, u32[]{:S(2)}) async-start(bf16[32,32,256]{2,1,0:T(8,128)(2,1)} %bitcast.159), calls=%async_computation.3 | async-start | bytes 1048576 | tf_op jit(solution)/shard_map/all_to_all | solution.py:1162
  444.6 20.3 %collective-permute-start.66 = (bf16[288,1024]{1,0:T(8,128)(2,1)}, bf16[288,1024]{1,0:T(8,128)(2,1)}, u32[]{:S(2)}, u32[]{:S(2)}) collective-permute-start(bf16[288,1024]{1,0:T(8,128)(2,1)} %add_convert_fusion.22), channel_id=1, source_target_pairs={{4,0},{5,1},{6,2},{7,3},{8,4},{9,5},{10,6},{11,7},{12,8},{13,9},{1... | collective-permute-start | bytes 1769480 | tf_op jit(solution)/shard_map/ppermute | solution.py:1036
  450.3 33.6 %all-to-all-start.4 = ((bf16[8,32,1152]{2,1,0:T(8,128)(2,1)}), bf16[8,32,1152]{2,1,0:T(8,128)(2,1)S(1)}, u32[]{:S(2)}, u32[]{:S(2)}) async-start(bf16[8,32,1152]{2,1,0:T(8,128)(2,1)} %add_convert_fusion.18), calls=%async_computation.4 | async-start | bytes 1179648 | tf_op jit(solution)/shard_map/all_to_all | solution.py:1158
  (101 other events, 1057.7 us)
Sparse Core Ops, SparseCore 0:
  62.0 92.4 all-gather.2

commit v2 on v1

--- a/solution.py
+++ b/solution.py
@@ -1162,14 +1162,15 @@
     head_grad = lax.all_to_all(head_grad, ("dp", "ep"), split_axis=0, concat_axis=0, tiled=True)
     totals, received = {}, None
 
-    def chip_of(d):
+    def chip_of(d, *earlier):
         half = 0 if d in halves[0] else 1
         at = halves[half].index(d)
-        return [add_low(near[half][at, y], got[half][at, y]) for y in range(ys)]
+        mine, theirs = phase(near[half], got[half], *earlier)[:2]
+        return [add_low(mine[at, y], theirs[at, y]) for y in range(ys)]
 
     chip = chip_of(turn_order[0])
     for k, d in enumerate(turn_order):
-        ahead = chip_of(turn_order[k + 1]) if k + 1 < len(turn_order) else []
+        ahead = chip_of(turn_order[k + 1], *chip) if k + 1 < len(turn_order) else []
         moved = [move(chip[y], True, dy=y) for y in range(1, ys)]
         if k:
             last = totals[turn_order[k - 1]]

time: 505 us -> 505 us (level)
    convert_element_type x25 -> x26, other arithmetic: 34.5 us -> 37 us  [add_low(): return total.astype(bf16)]
  transfers between devices with their start and end apart: 75 -> 75, of which waited for: 33 -> 32; matrix products, arithmetic and copies ran while one was open for 16% -> 16% of each run, Pallas kernels for 29% -> 29%
where the time goes in v2:
time: 505 us; the launch traced here: 497 us
  Pallas kernels  150 us (30%)
  waiting for transfers between devices  146 us (29%)
  starting transfers between devices  97.6 us (19%)
  other arithmetic  62.7 us (12%)
  local copies, waits for them, and re-layouts  24.9 us (5%)
  between operations  15.7 us (3%)
    ppermute x54, waiting for transfers between devices, move(): lax.ppermute(x, 'ep', (send_to if sender else fetch_from)(ep, **offset))  79.6 us
    ppermute x54, starting transfers between devices, move(): lax.ppermute(x, 'ep', (send_to if sender else fetch_from)(ep, **offset))  49.1 us
    pallas_call x4, Pallas kernels, experts(): pl.pallas_call(functools.partial(expert_kernel, place, cap, zs, dz, first...  48.9 us
    convert_element_type x26, other arithmetic, add_low(): return total.astype(bf16)  37 us
    all_to_all x1, waiting for transfers between devices, body(): recv = lax.all_to_all(made, 'ep', split_axis=0, concat_axis=0, tiled=True)  24.5 us
    ppermute x9, waiting for transfers between devices, hop(): return lax.ppermute(value, 'ep', fetch_from(ep, dz=1))  22.4 us
    pallas_call x4, Pallas kernels, project(): pl.pallas_call(functools.partial(project_kernel, place, carried is not No...  21.7 us
    pallas_call x1, Pallas kernels, back(): pl.pallas_call(functools.partial(back_kernel, replicas), grid=(seqs,), ou...  17.6 us
  transfers between devices with their start and end apart: 75, of which 32 were waited for; matrix products, arithmetic and copies ran while one was open for 16% of the time, Pallas kernels for 29%

profile of v2, /device:TPU:8, one launch (start us, length us, event | category | flops | bytes accessed | tf_op | source)
XLA Modules:
  0.0 496.6 jit_solution(4631749060707299017)
XLA Ops:
  14.1 5.9 %all-to-all-start = ((bf16[32,32,256]{2,1,0:T(8,128)(2,1)}), bf16[32,32,256]{2,1,0:T(8,128)(2,1)S(1)}, u32[]{:S(2)}, u32[]{:S(2)}) async-start(bf16[32,32,256]{2,1,0:T(8,128)(2,1)} %bitcast.9), calls=%async_computation | async-start | bytes 1048576 | tf_op jit(solution)/shard_map/all_to_all | solution.py:923
  22.9 7.0 %collective-permute-start.2 = (bf16[288,1024]{1,0:T(8,128)(2,1)}, bf16[288,1024]{1,0:T(8,128)(2,1)}, u32[]{:S(2)}, u32[]{:S(2)}) collective-permute-start(bf16[288,1024]{1,0:T(8,128)(2,1)} %collective-permute-done.refs_0_), channel_id=1, source_target_pairs={{4,0},{5,1},{6,2},{7,3},{8,4},{9,5},{10,6},{11,7},{12,8},{13,9},{1... | collective-permute-start | bytes 1769480 | tf_op jit(solution)/shard_map/ppermute | solution.py:971
  40.6 6.0 %collective-permute-done.2.refs_0_ = bf16[288,1024]{1,0:T(8,128)(2,1)} collective-permute-done((bf16[288,1024]{1,0:T(8,128)(2,1)}, bf16[288,1024]{1,0:T(8,128)(2,1)}, u32[]{:S(2)}, u32[]{:S(2)}) %collective-permute-start.2) | collective-permute-done | bytes 589856 | tf_op jit(solution)/shard_map/ppermute | solution.py:971
  50.9 5.5 %project_in.4 = (bf16[4,4,288,1024]{3,2,1,0:T(8,128)(2,1)}, bf16[4,4,288,256]{3,2,1,0:T(8,128)(2,1)}) custom-call(s32[5]{0:T(128)} %pad_add_fusion.meta, bf16[288,1024]{1,0:T(8,128)(2,1)} %bitcast.refs_0_.hid_ref, bf16[288,1024]{1,0:T(8,128)(2,1)} %collective-permute-done.1.refs_1_, bf16[288,1024]{1,0:T(8,128)(2,1)} %collective-permute-done.4.refs_2_, ...), custom_call_target="tpu_custom_call" | custom-call | flops 603979776 | bytes 4718592 | tf_op jit(solution)/shard_map/project_in/pallas_call | solution.py:119
  56.3 5.4 %collective-permute-done.6.refs_0_ = bf16[288,1024]{1,0:T(8,128)(2,1)S(1)} collective-permute-done((bf16[288,1024]{1,0:T(8,128)(2,1)}, bf16[288,1024]{1,0:T(8,128)(2,1)S(1)}, u32[]{:S(2)}, u32[]{:S(2)}) %collective-permute-start.6) | collective-permute-done | bytes 589856 | tf_op jit(solution)/shard_map/ppermute | solution.py:971
  70.6 5.6 %project_in.5 = (bf16[4,4,288,1024]{3,2,1,0:T(8,128)(2,1)}, bf16[4,4,288,256]{3,2,1,0:T(8,128)(2,1)}) custom-call(s32[5]{0:T(128)} %pad_add_fusion.meta, bf16[288,1024]{1,0:T(8,128)(2,1)} %collective-permute-done.refs_0_, bf16[288,1024]{1,0:T(8,128)(2,1)} %collective-permute-done.3.refs_1_, ...), custom_call_target="tpu_custom_call", output_to_operand_aliasing={{0}: (9, {}), {1}: (10, {})} | custom-call | flops 603979776 | bytes 4718592 | tf_op jit(solution)/shard_map/project_in/pallas_call | solution.py:119
  83.1 5.4 %project_in.6 = (bf16[4,4,288,1024]{3,2,1,0:T(8,128)(2,1)}, bf16[4,4,288,256]{3,2,1,0:T(8,128)(2,1)}) custom-call(s32[5]{0:T(128)} %pad_add_fusion.meta, bf16[288,1024]{1,0:T(8,128)(2,1)} %collective-permute-done.2.refs_0_, bf16[288,1024]{1,0:T(8,128)(2,1)} %copy-done.21, ...), custom_call_target="tpu_custom_call", output_to_operand_aliasing={{0}: (9, {}), {1}: (10, {})} | custom-call | flops 603979776 | bytes 4718592 | tf_op jit(solution)/shard_map/project_in/pallas_call | solution.py:119
  90.7 5.3 %project_in.7 = (bf16[4,4,288,1024]{3,2,1,0:T(8,128)(2,1)}, bf16[4,4,288,256]{3,2,1,0:T(8,128)(2,1)}) custom-call(s32[5]{0:T(128)} %pad_add_fusion.meta, bf16[288,1024]{1,0:T(8,128)(2,1)} %copy-done.20, bf16[288,1024]{1,0:T(8,128)(2,1)} %copy-done.22, bf16[288,1024]{1,0:T(8,128)(2,1)} %copy-done.28, ...), custom_call_target="tpu_custom_call", output_to_operand_aliasing={{0}: (9, {}), {1}: (10, {})} | custom-call | flops 603979776 | bytes 4718592 | tf_op jit(solution)/shard_map/project_in/pallas_call | solution.py:119
  98.2 11.2 %attend_forward.1 = (bf16[16,144,128]{2,1,0:T(8,128)(2,1)}, bf16[3,1536,128]{2,1,0:T(8,128)(2,1)}, bf16[3,1536,128]{2,1,0:T(8,128)(2,1)}, bf16[3,128,1536]{2,1,0:T(8,128)(2,1)}, f32[3,72,1536]{2,1,0:T(8,128)}) custom-call(s32[12]{0:T(128)} %concatenate.34.meta, bf16[4,4,288,256]{3,2,1,0:T(8,128)(2,1)} %get-tuple-element.369.qkv_ref), custom_call_target="tpu_custom_call" | custom-call | flops 3623878656 | bytes 4718592 | tf_op jit(solution)/shard_map/attend_forward/pallas_call | solution.py:220
  111.6 7.1 %all-to-all-start.1 = ((bf16[16,144,128]{2,1,0:T(8,128)(2,1)}), bf16[16,144,128]{2,1,0:T(8,128)(2,1)}, u32[]{:S(2)}, u32[]{:S(2)}) async-start(bf16[16,144,128]{2,1,0:T(8,128)(2,1)} %get-tuple-element.372), calls=%async_computation.1 | async-start | bytes 1179648 | tf_op jit(solution)/shard_map/all_to_all | solution.py:1015
  123.1 24.5 %all-to-all-done.1.recv_ref = bf16[16,144,128]{2,1,0:T(8,128)(2,1)} async-done(((bf16[16,144,128]{2,1,0:T(8,128)(2,1)}), bf16[16,144,128]{2,1,0:T(8,128)(2,1)}, u32[]{:S(2)}, u32[]{:S(2)}) %all-to-all-start.1) | async-done | bytes 589856 | tf_op jit(solution)/shard_map/all_to_all | solution.py:1015
  147.5 4.4 project_out.1
  155.8 12.8 %collective-permute-done.21.refs_0_ = bf16[288,1024]{1,0:T(8,128)(2,1)S(1)} collective-permute-done((bf16[288,1024]{1,0:T(8,128)(2,1)}, bf16[288,1024]{1,0:T(8,128)(2,1)S(1)}, u32[]{:S(2)}, u32[]{:S(2)}) %collective-permute-start.21) | collective-permute-done | bytes 589856 | tf_op jit(solution)/shard_map/ppermute | solution.py:971
  173.6 10.9 %collective-permute-done.23.refs_0_ = bf16[288,1024]{1,0:T(8,128)(2,1)S(1)} collective-permute-done((bf16[288,1024]{1,0:T(8,128)(2,1)S(1)}, bf16[288,1024]{1,0:T(8,128)(2,1)S(1)}, u32[]{:S(2)}, u32[]{:S(2)}) %collective-permute-start.23) | collective-permute-done | bytes 589856 | tf_op jit(solution)/shard_map/ppermute | solution.py:971
  192.0 12.2 %experts.4 = (bf16[2,304,1024]{2,1,0:T(8,128)(2,1)}, bf16[2,304,1024]{2,1,0:T(8,128)(2,1)}, bf16[4,2,288,1024]{3,2,1,0:T(8,128)(2,1)}, bf16[4,2,288,1024]{3,2,1,...) custom-call(s32[6]{0:T(128)} %pad_add_fusion.2.meta, ...), custom_call_target="tpu_custom_call" | custom-call | flops 4831838208 | bytes 7077888 | tf_op jit(solution)/shard_map/experts/pallas_call | solution.py:456
  205.2 12.4 %experts.5 = (bf16[2,304,1024]{2,1,0:T(8,128)(2,1)}, bf16[2,304,1024]{2,1,0:T(8,128)(2,1)}, bf16[4,2,288,1024]{3,2,1,0:T(8,128)(2,1)}, bf16[4,2,288,1024]{3,2,1,...) custom-call(s32[6]{0:T(128)} %pad_add_fusion.2.meta, ...), custom_call_target="tpu_custom_call", output_to_operand_aliasing={{2}: (9, {}), {3}: (10, {}), {4}: (11, {}), {5}: (12, {}), ... | custom-call | flops 4831838208 | bytes 7077888 | tf_op jit(solution)/shard_map/experts/pallas_call | solution.py:456
  222.6 12.2 %experts.6 = (bf16[2,304,1024]{2,1,0:T(8,128)(2,1)}, bf16[2,304,1024]{2,1,0:T(8,128)(2,1)}, bf16[4,2,288,1024]{3,2,1,0:T(8,128)(2,1)}, bf16[4,2,288,1024]{3,2,1,...) custom-call(s32[6]{0:T(128)} %pad_add_fusion.2.meta, ...), custom_call_target="tpu_custom_call", output_to_operand_aliasing={{2}: (9, {}), {3}: (10, {}), {4}: (11, {}), {5}: (12, {}), ... | custom-call | flops 4831838208 | bytes 7077888 | tf_op jit(solution)/shard_map/experts/pallas_call | solution.py:456
  240.6 12.3 %experts.7 = (bf16[2,304,1024]{2,1,0:T(8,128)(2,1)}, bf16[2,304,1024]{2,1,0:T(8,128)(2,1)}, bf16[4,2,288,1024]{3,2,1,0:T(8,128)(2,1)}, bf16[4,2,288,1024]{3,2,1,...) custom-call(s32[6]{0:T(128)} %pad_add_fusion.2.meta, ...), custom_call_target="tpu_custom_call", output_to_operand_aliasing={{2}: (9, {}), {3}: (10, {}), {4}: (11, {}), {5}: (12, {}), ... | custom-call | flops 4831838208 | bytes 7077888 | tf_op jit(solution)/shard_map/experts/pallas_call | solution.py:456
  262.3 15.2 %expert_grads.1 = (bf16[384,1024]{1,0:T(8,128)(2,1)}, bf16[384,1024]{1,0:T(8,128)(2,1)}, bf16[384,1024]{1,0:T(8,128)(2,1)}, bf16[384,1024]{1,0:T(8,128)(2,1)}) custom-call(bf16[4,576,1024]{2,1,0:T(8,128)(2,1)} %get-tuple-element.483.x_ref, bf16[4,576,1024]{2,1,0:T(8,128)(2,1)} %get-tuple-element.486.both_ref, ...), custom_call_target="tpu_custom_call" | custom-call | flops 7247757312 | bytes 18874368 | tf_op jit(solution)/shard_map/expert_grads/pallas_call | solution.py:729
  300.8 10.9 %collective-permute-done.48 = bf16[1,288,1024]{2,1,0:T(8,128)(2,1)S(1)} collective-permute-done((bf16[1,288,1024]{2,1,0:T(8,128)(2,1)S(1)}, bf16[1,288,1024]{2,1,0:T(8,128)(2,1)S(1)}, u32[]{:S(2)}, u32[]{:S(2)}) %collective-permute-start.48) | collective-permute-done | bytes 589856 | tf_op jit(solution)/shard_map/ppermute | solution.py:971
  315.6 6.1 %turn_back.1 = (f32[288,1024]{1,0:T(8,128)}, bf16[288,1024]{1,0:T(8,128)(2,1)}, bf16[16,144,128]{2,1,0:T(8,128)(2,1)}, f32[288,128]{1,0:T(8,128)}, f32[1,1024]{1,0:T(1,128)}) custom-call(s32[4]{0:T(128)} %pad_add_fusion.1.meta, bf16[304,1024]{1,0:T(8,128)(2,1)} %add_convert_fusion.13.refs_0_, bf16[304,1024]{1,0:T(8,128)(2,1)} %copy-done.19, ...), custom_call_target="tpu_custom_call" | custom-call | flops 1207959552 | bytes 4194304 | tf_op jit(solution)/shard_map/turn_back/pallas_call | solution.py:562
  321.7 6.6 %all-to-all-start.2 = ((bf16[16,144,128]{2,1,0:T(8,128)(2,1)}), bf16[16,144,128]{2,1,0:T(8,128)(2,1)}, u32[]{:S(2)}, u32[]{:S(2)}) async-start(bf16[16,144,128]{2,1,0:T(8,128)(2,1)} %get-tuple-element.522), calls=%async_computation.2 | async-start | bytes 1179648 | tf_op jit(solution)/shard_map/all_to_all | solution.py:1111
  329.1 4.6 late_grads.1
  337.6 10.5 %collective-permute-done.51 = bf16[384,1024]{1,0:T(8,128)(2,1)} collective-permute-done((bf16[384,1024]{1,0:T(8,128)(2,1)}, bf16[384,1024]{1,0:T(8,128)(2,1)}, u32[]{:S(2)}, u32[]{:S(2)}) %collective-permute-start.51) | collective-permute-done | bytes 786464 | tf_op jit(solution)/shard_map/ppermute | solution.py:1039
  353.1 17.6 %attend_backward.1.dqkv_ref = bf16[4,4,288,256]{3,2,1,0:T(8,128)(2,1)} custom-call(s32[12]{0:T(128)} %concatenate.34.meta, bf16[16,144,128]{2,1,0:T(8,128)(2,1)} %all-to-all-done.2.grad_ref, bf16[3,1536,128]{2,1,0:T(8,128)(2,1)} %get-tuple-element.540.qk_ref, bf16[3,1536,128]{2,1,0:T(8,128)(2,1)} %get-tuple-element.541.v_ref, ...), custom_call_target="tpu_custom_call" | custom-call | flops 9059696640 | bytes 7077888 | tf_op jit(solution)/shard_map/attend_backward/pallas_call | solution.py:671
  370.8 4.9 spread.2
  387.1 7.8 %head_grads.1 = bf16[1024,256]{1,0:T(8,128)(2,1)} custom-call(bf16[4,4,288,256]{3,2,1,0:T(8,128)(2,1)} %attend_backward.1.dqkv_ref, bf16[4,4,288,1024]{3,2,1,0:T(8,128)(2,1)} %get-tuple-element.567.normed_ref), custom_call_target="tpu_custom_call" | custom-call | flops 2415919104 | bytes 9437184 | tf_op jit(solution)/shard_map/head_grads/pallas_call | solution.py:789
  420.6 4.3 collective-permute-done.62
  449.2 5.5 %all-to-all-start.4 = ((bf16[8,32,1152]{2,1,0:T(8,128)(2,1)}), bf16[8,32,1152]{2,1,0:T(8,128)(2,1)S(1)}, u32[]{:S(2)}, u32[]{:S(2)}) async-start(bf16[8,32,1152]{2,1,0:T(8,128)(2,1)} %add_convert_fusion.18), calls=%async_computation.4 | async-start | bytes 1179648 | tf_op jit(solution)/shard_map/all_to_all | solution.py:1158
  456.2 7.0 %collective-permute-done.66 = bf16[288,1024]{1,0:T(8,128)(2,1)S(1)} collective-permute-done((bf16[288,1024]{1,0:T(8,128)(2,1)}, bf16[288,1024]{1,0:T(8,128)(2,1)S(1)}, u32[]{:S(2)}, u32[]{:S(2)}) %collective-permute-start.66) | collective-permute-done | bytes 589856 | tf_op jit(solution)/shard_map/ppermute | solution.py:1036
  467.2 7.1 %collective-permute-done.67 = bf16[288,1024]{1,0:T(8,128)(2,1)} collective-permute-done((bf16[288,1024]{1,0:T(8,128)(2,1)S(1)}, bf16[288,1024]{1,0:T(8,128)(2,1)}, u32[]{:S(2)}, u32[]{:S(2)}) %collective-permute-start.67) | collective-permute-done | bytes 589856 | tf_op jit(solution)/shard_map/ppermute | solution.py:971
  474.3 7.1 %collective-permute-done.68.refs_4_ = bf16[288,1024]{1,0:T(8,128)(2,1)S(1)} collective-permute-done((bf16[288,1024]{1,0:T(8,128)(2,1)}, bf16[288,1024]{1,0:T(8,128)(2,1)S(1)}, u32[]{:S(2)}, u32[]{:S(2)}) %collective-permute-start.68) | collective-permute-done | bytes 589856 | tf_op jit(solution)/shard_map/ppermute | solution.py:1036
  (373 shorter events, 199.9 us)
Async XLA Ops:
  14.1 34.6 %all-to-all-start = ((bf16[32,32,256]{2,1,0:T(8,128)(2,1)}), bf16[32,32,256]{2,1,0:T(8,128)(2,1)S(1)}, u32[]{:S(2)}, u32[]{:S(2)}) async-start(bf16[32,32,256]{2,1,0:T(8,128)(2,1)} %bitcast.9), calls=%async_computation | async-start | bytes 1048576 | tf_op jit(solution)/shard_map/all_to_all | solution.py:923
  20.0 172.0 %all-gather.3.cloned.1.call-start = ((), (), s32[]{:S(2)}) async-start(), calls=%async_computation.5 | async-start | bytes 10584064 | tf_op jit(solution)/shard_map/all_gather | solution.py:1008
  22.9 23.7 %collective-permute-start.2 = (bf16[288,1024]{1,0:T(8,128)(2,1)}, bf16[288,1024]{1,0:T(8,128)(2,1)}, u32[]{:S(2)}, u32[]{:S(2)}) collective-permute-start(bf16[288,1024]{1,0:T(8,128)(2,1)} %collective-permute-done.refs_0_), channel_id=1, source_target_pairs={{4,0},{5,1},{6,2},{7,3},{8,4},{9,5},{10,6},{11,7},{12,8},{13,9},{1... | collective-permute-start | bytes 1769480 | tf_op jit(solution)/shard_map/ppermute | solution.py:971
  29.9 16.7 %collective-permute-start.3 = (bf16[288,1024]{1,0:T(8,128)(2,1)}, bf16[288,1024]{1,0:T(8,128)(2,1)}, u32[]{:S(2)}, u32[]{:S(2)}) collective-permute-start(bf16[288,1024]{1,0:T(8,128)(2,1)} %collective-permute-done.refs_0_), channel_id=1, source_target_pairs={{2,0},{3,1},{0,2},{1,3},{6,4},{7,5},{4,6},{5,7},{10,8},{11,9},{8,1... | collective-permute-start | bytes 1769480 | tf_op jit(solution)/shard_map/ppermute | solution.py:971
  61.9 18.0 %collective-permute-start.10 = (bf16[288,1024]{1,0:T(8,128)(2,1)S(1)}, bf16[288,1024]{1,0:T(8,128)(2,1)S(1)}, u32[]{:S(2)}, u32[]{:S(2)}) collective-permute-start(bf16[288,1024]{1,0:T(8,128)(2,1)S(1)} %collective-permute-done.6.refs_0_), channel_id=1, source_target_pairs={{2,0},{3,1},{0,2},{1,3},{6,4},{7,5},{4,6},{5,7},{10,8},{11,9},{8,1... | collective-permute-start | bytes 1769480 | tf_op jit(solution)/shard_map/ppermute | solution.py:971
  111.6 35.9 %all-to-all-start.1 = ((bf16[16,144,128]{2,1,0:T(8,128)(2,1)}), bf16[16,144,128]{2,1,0:T(8,128)(2,1)}, u32[]{:S(2)}, u32[]{:S(2)}) async-start(bf16[16,144,128]{2,1,0:T(8,128)(2,1)} %get-tuple-element.372), calls=%async_computation.1 | async-start | bytes 1179648 | tf_op jit(solution)/shard_map/all_to_all | solution.py:1015
  152.0 16.7 %collective-permute-start.21 = (bf16[288,1024]{1,0:T(8,128)(2,1)}, bf16[288,1024]{1,0:T(8,128)(2,1)S(1)}, u32[]{:S(2)}, u32[]{:S(2)}) collective-permute-start(bf16[288,1024]{1,0:T(8,128)(2,1)} %get-tuple-element.531.refs_0_.pay_ref), channel_id=1, source_target_pairs={{4,0},{5,1},{6,2},{7,3},{8,4},{9,5},{10,6},{11,7},{12,8},{13,9},{1... | collective-permute-start | bytes 1769480 | tf_op jit(solution)/shard_map/ppermute | solution.py:971
  152.0 17.7 %collective-permute-start.22 = (bf16[288,1024]{1,0:T(8,128)(2,1)}, bf16[288,1024]{1,0:T(8,128)(2,1)S(1)}, u32[]{:S(2)}, u32[]{:S(2)}) collective-permute-start(bf16[288,1024]{1,0:T(8,128)(2,1)} %get-tuple-element.531.refs_0_.pay_ref), channel_id=1, source_target_pairs={{2,0},{3,1},{0,2},{1,3},{6,4},{7,5},{4,6},{5,7},{10,8},{11,9},{8,1... | collective-permute-start | bytes 1769480 | tf_op jit(solution)/shard_map/ppermute | solution.py:971
  186.9 17.3 %collective-permute-start.27 = (bf16[288,1024]{1,0:T(8,128)(2,1)S(1)}, bf16[288,1024]{1,0:T(8,128)(2,1)S(1)}, u32[]{:S(2)}, u32[]{:S(2)}) collective-permute-start(bf16[288,1024]{1,0:T(8,128)(2,1)S(1)} %collective-permute-done.23.refs_0_), channel_id=1, source_target_pairs={{4,0},{5,1},{6,2},{7,3},{8,4},{9,5},{10,6},{11,7},{12,8},{13,9},{1... | collective-permute-start | bytes 1769480 | tf_op jit(solution)/shard_map/ppermute | solution.py:971
  221.1 17.0 %collective-permute-start.37 = (bf16[2,304,1024]{2,1,0:T(8,128)(2,1)}, bf16[2,304,1024]{2,1,0:T(8,128)(2,1)S(1)}, u32[]{:S(2)}, u32[]{:S(2)}) collective-permute-start(bf16[2,304,1024]{2,1,0:T(8,128)(2,1)} %get-tuple-element.432), channel_id=1, source_target_pairs={{0,1},{1,0},{2,3},{3,2},{4,5},{5,4},{6,7},{7,6},{8,9},{9,8},{10,11... | collective-permute-start | bytes 3735560 | tf_op jit(solution)/shard_map/ppermute | solution.py:971
  238.2 17.5 %collective-permute-start.39 = (bf16[2,304,1024]{2,1,0:T(8,128)(2,1)}, bf16[2,304,1024]{2,1,0:T(8,128)(2,1)S(1)}, u32[]{:S(2)}, u32[]{:S(2)}) collective-permute-start(bf16[2,304,1024]{2,1,0:T(8,128)(2,1)} %get-tuple-element.455), channel_id=1, source_target_pairs={{0,1},{1,0},{2,3},{3,2},{4,5},{5,4},{6,7},{7,6},{8,9},{9,8},{10,11... | collective-permute-start | bytes 3735560 | tf_op jit(solution)/shard_map/ppermute | solution.py:971
  255.7 21.8 %collective-permute-start.44 = (bf16[4,2,288,1024]{3,2,1,0:T(8,128)(2,1)}, bf16[4,2,288,1024]{3,2,1,0:T(8,128)(2,1)}, u32[]{:S(2)}, u32[]{:S(2)}) collective-permute-start(bf16[4,2,288,1024]{3,2,1,0:T(8,128)(2,1)} %get-tuple-element.482), channel_id=1, source_target_pairs={{0,1},{1,0},{2,3},{3,2},{4,5},{5,4},{6,7},{7,6},{8,9},{9,8},{10,11... | collective-permute-start | bytes 14155784 | tf_op jit(solution)/shard_map/ppermute | solution.py:971
  255.7 21.8 %collective-permute-start.41 = (bf16[2,304,1024]{2,1,0:T(8,128)(2,1)}, bf16[2,304,1024]{2,1,0:T(8,128)(2,1)S(1)}, u32[]{:S(2)}, u32[]{:S(2)}) collective-permute-start(bf16[2,304,1024]{2,1,0:T(8,128)(2,1)} %get-tuple-element.476), channel_id=1, source_target_pairs={{0,1},{1,0},{2,3},{3,2},{4,5},{5,4},{6,7},{7,6},{8,9},{9,8},{10,11... | collective-permute-start | bytes 3735560 | tf_op jit(solution)/shard_map/ppermute | solution.py:971
  257.5 20.0 %collective-permute-start.42 = (bf16[304,1024]{1,0:T(8,128)(2,1)}, bf16[304,1024]{1,0:T(8,128)(2,1)}, u32[]{:S(2)}, u32[]{:S(2)}) collective-permute-start(bf16[304,1024]{1,0:T(8,128)(2,1)} %get-tuple-element.749), channel_id=1, source_target_pairs={{0,2},{1,3},{2,0},{3,1},{4,6},{5,7},{6,4},{7,5},{8,10},{9,11},{10,... | collective-permute-start | bytes 1867784 | tf_op jit(solution)/shard_map/ppermute | solution.py:971
  260.1 17.4 %collective-permute-start.43 = (bf16[304,1024]{1,0:T(8,128)(2,1)}, bf16[304,1024]{1,0:T(8,128)(2,1)}, u32[]{:S(2)}, u32[]{:S(2)}) collective-permute-start(bf16[304,1024]{1,0:T(8,128)(2,1)} %add_convert_fusion.10), channel_id=1, source_target_pairs={{4,0},{5,1},{6,2},{7,3},{8,4},{9,5},{10,6},{11,7},{12,8},{13,9},{1... | collective-permute-start | bytes 1867784 | tf_op jit(solution)/shard_map/ppermute | solution.py:1036
  296.6 17.8 %collective-permute-start.49 = (bf16[384,1024]{1,0:T(8,128)(2,1)S(1)}, bf16[384,1024]{1,0:T(8,128)(2,1)S(1)}, u32[]{:S(2)}, u32[]{:S(2)}) collective-permute-start(bf16[384,1024]{1,0:T(8,128)(2,1)S(1)} %copy-done.12), channel_id=1, source_target_pairs={{0,16},{16,0},{1,17},{17,1},{2,18},{18,2},{3,19},{19,3},{4,20},{20... | collective-permute-start | bytes 2359304 | tf_op jit(solution)/shard_map/ppermute | solution.py:1039
  315.3 32.9 %collective-permute-start.50 = (bf16[2,288,1024]{2,1,0:T(8,128)(2,1)}, bf16[2,288,1024]{2,1,0:T(8,128)(2,1)}, u32[]{:S(2)}, u32[]{:S(2)}) collective-permute-start(bf16[2,288,1024]{2,1,0:T(8,128)(2,1)} %add_convert_fusion.2), channel_id=1, source_target_pairs={{0,2},{1,3},{2,0},{3,1},{4,6},{5,7},{6,4},{7,5},{8,10},{9,11},{10,... | collective-permute-start | bytes 3538952 | tf_op jit(solution)/shard_map/ppermute | solution.py:971
  321.7 26.5 %all-to-all-start.2 = ((bf16[16,144,128]{2,1,0:T(8,128)(2,1)}), bf16[16,144,128]{2,1,0:T(8,128)(2,1)}, u32[]{:S(2)}, u32[]{:S(2)}) async-start(bf16[16,144,128]{2,1,0:T(8,128)(2,1)} %get-tuple-element.522), calls=%async_computation.2 | async-start | bytes 1179648 | tf_op jit(solution)/shard_map/all_to_all | solution.py:1111
  328.3 19.9 %collective-permute-start.51 = (bf16[384,1024]{1,0:T(8,128)(2,1)}, bf16[384,1024]{1,0:T(8,128)(2,1)}, u32[]{:S(2)}, u32[]{:S(2)}) collective-permute-start(bf16[384,1024]{1,0:T(8,128)(2,1)} %get-tuple-element.620), channel_id=1, source_target_pairs={{0,16},{16,0},{1,17},{17,1},{2,18},{18,2},{3,19},{19,3},{4,20},{20... | collective-permute-start | bytes 2359304 | tf_op jit(solution)/shard_map/ppermute | solution.py:1039
  348.2 22.6 %collective-permute-start.54 = (bf16[2,8,32,1152]{3,2,1,0:T(8,128)(2,1)}, bf16[2,8,32,1152]{3,2,1,0:T(8,128)(2,1)S(1)}, u32[]{:S(2)}, u32[]{:S(2)}) collective-permute-start(bf16[2,8,32,1152]{3,2,1,0:T(8,128)(2,1)} %get-tuple-element.550), channel_id=1, source_target_pairs={{0,1},{1,0},{2,3},{3,2},{4,5},{5,4},{6,7},{7,6},{8,9},{9,8},{10,11... | collective-permute-start | bytes 3538952 | tf_op jit(solution)/shard_map/ppermute | solution.py:971
  348.2 22.5 %collective-permute-start.52 = (bf16[1,288,1024]{2,1,0:T(8,128)(2,1)}, bf16[1,288,1024]{2,1,0:T(8,128)(2,1)S(1)}, u32[]{:S(2)}, u32[]{:S(2)}) collective-permute-start(bf16[1,288,1024]{2,1,0:T(8,128)(2,1)} %get-tuple-element.547), channel_id=1, source_target_pairs={{0,2},{1,3},{2,0},{3,1},{4,6},{5,7},{6,4},{7,5},{8,10},{9,11},{10,... | collective-permute-start | bytes 1769480 | tf_op jit(solution)/shard_map/ppermute | solution.py:971
  349.7 21.0 %collective-permute-start.53 = (bf16[288,1024]{1,0:T(8,128)(2,1)}, bf16[288,1024]{1,0:T(8,128)(2,1)S(1)}, u32[]{:S(2)}, u32[]{:S(2)}) collective-permute-start(bf16[288,1024]{1,0:T(8,128)(2,1)} %bitcast.57), channel_id=1, source_target_pairs={{4,0},{5,1},{6,2},{7,3},{8,4},{9,5},{10,6},{11,7},{12,8},{13,9},{1... | collective-permute-start | bytes 1769480 | tf_op jit(solution)/shard_map/ppermute | solution.py:1036
  350.5 20.3 %collective-permute-start.55 = (bf16[384,1024]{1,0:T(8,128)(2,1)}, bf16[384,1024]{1,0:T(8,128)(2,1)S(1)}, u32[]{:S(2)}, u32[]{:S(2)}) collective-permute-start(bf16[384,1024]{1,0:T(8,128)(2,1)} %get-tuple-element.622), channel_id=1, source_target_pairs={{0,16},{16,0},{1,17},{17,1},{2,18},{18,2},{3,19},{19,3},{4,20},{20... | collective-permute-start | bytes 2359304 | tf_op jit(solution)/shard_map/ppermute | solution.py:1039
  375.7 21.4 %collective-permute-start.56 = (bf16[2,2,288,1024]{3,2,1,0:T(8,128)(2,1)}, bf16[2,2,288,1024]{3,2,1,0:T(8,128)(2,1)}, u32[]{:S(2)}, u32[]{:S(2)}) collective-permute-start(bf16[2,2,288,1024]{3,2,1,0:T(8,128)(2,1)} %get-tuple-element.561), channel_id=1, source_target_pairs={{0,1},{1,0},{2,3},{3,2},{4,5},{5,4},{6,7},{7,6},{8,9},{9,8},{10,11... | collective-permute-start | bytes 7077896 | tf_op jit(solution)/shard_map/ppermute | solution.py:971
  378.1 17.0 %collective-permute-start.57 = (bf16[288,1024]{1,0:T(8,128)(2,1)}, bf16[288,1024]{1,0:T(8,128)(2,1)S(1)}, u32[]{:S(2)}, u32[]{:S(2)}) collective-permute-start(bf16[288,1024]{1,0:T(8,128)(2,1)} %fusion.5), channel_id=1, source_target_pairs={{4,0},{5,1},{6,2},{7,3},{8,4},{9,5},{10,6},{11,7},{12,8},{13,9},{1... | collective-permute-start | bytes 1769480 | tf_op jit(solution)/shard_map/ppermute | solution.py:1036
  397.2 27.8 %collective-permute-start.59 = (bf16[2,2,288,1024]{3,2,1,0:T(8,128)(2,1)}, bf16[2,2,288,1024]{3,2,1,0:T(8,128)(2,1)}, u32[]{:S(2)}, u32[]{:S(2)}) collective-permute-start(bf16[2,2,288,1024]{3,2,1,0:T(8,128)(2,1)} %get-tuple-element.578), channel_id=1, source_target_pairs={{0,1},{1,0},{2,3},{3,2},{4,5},{5,4},{6,7},{7,6},{8,9},{9,8},{10,11... | collective-permute-start | bytes 7077896 | tf_op jit(solution)/shard_map/ppermute | solution.py:971
  399.9 17.7 %collective-permute-start.60 = (bf16[288,1024]{1,0:T(8,128)(2,1)}, bf16[288,1024]{1,0:T(8,128)(2,1)}, u32[]{:S(2)}, u32[]{:S(2)}) collective-permute-start(bf16[288,1024]{1,0:T(8,128)(2,1)} %get-tuple-element.737), channel_id=1, source_target_pairs={{0,2},{1,3},{2,0},{3,1},{4,6},{5,7},{6,4},{7,5},{8,10},{9,11},{10,... | collective-permute-start | bytes 1769480 | tf_op jit(solution)/shard_map/ppermute | solution.py:971
  401.5 19.1 %collective-permute-start.61 = (bf16[288,1024]{1,0:T(8,128)(2,1)}, bf16[288,1024]{1,0:T(8,128)(2,1)}, u32[]{:S(2)}, u32[]{:S(2)}) collective-permute-start(bf16[288,1024]{1,0:T(8,128)(2,1)} %fusion.3), channel_id=1, source_target_pairs={{4,0},{5,1},{6,2},{7,3},{8,4},{9,5},{10,6},{11,7},{12,8},{13,9},{1... | collective-permute-start | bytes 1769480 | tf_op jit(solution)/shard_map/ppermute | solution.py:1036
  402.1 22.9 %collective-permute-start.62 = (bf16[384,1024]{1,0:T(8,128)(2,1)}, bf16[384,1024]{1,0:T(8,128)(2,1)}, u32[]{:S(2)}, u32[]{:S(2)}) collective-permute-start(bf16[384,1024]{1,0:T(8,128)(2,1)} %get-tuple-element.585), channel_id=1, source_target_pairs={{0,16},{16,0},{1,17},{17,1},{2,18},{18,2},{3,19},{19,3},{4,20},{20... | collective-permute-start | bytes 2359304 | tf_op jit(solution)/shard_map/ppermute | solution.py:1039
  403.2 46.0 %all-to-all-start.3 = ((bf16[32,32,256]{2,1,0:T(8,128)(2,1)}), bf16[32,32,256]{2,1,0:T(8,128)(2,1)S(1)}, u32[]{:S(2)}, u32[]{:S(2)}) async-start(bf16[32,32,256]{2,1,0:T(8,128)(2,1)} %bitcast.59), calls=%async_computation.3 | async-start | bytes 1048576 | tf_op jit(solution)/shard_map/all_to_all | solution.py:1162
  443.4 19.7 %collective-permute-start.66 = (bf16[288,1024]{1,0:T(8,128)(2,1)}, bf16[288,1024]{1,0:T(8,128)(2,1)S(1)}, u32[]{:S(2)}, u32[]{:S(2)}) collective-permute-start(bf16[288,1024]{1,0:T(8,128)(2,1)} %add_convert_fusion.22), channel_id=1, source_target_pairs={{4,0},{5,1},{6,2},{7,3},{8,4},{9,5},{10,6},{11,7},{12,8},{13,9},{1... | collective-permute-start | bytes 1769480 | tf_op jit(solution)/shard_map/ppermute | solution.py:1036
  449.2 34.6 %all-to-all-start.4 = ((bf16[8,32,1152]{2,1,0:T(8,128)(2,1)}), bf16[8,32,1152]{2,1,0:T(8,128)(2,1)S(1)}, u32[]{:S(2)}, u32[]{:S(2)}) async-start(bf16[8,32,1152]{2,1,0:T(8,128)(2,1)} %add_convert_fusion.18), calls=%async_computation.4 | async-start | bytes 1179648 | tf_op jit(solution)/shard_map/all_to_all | solution.py:1158
  (105 other events, 1076.3 us)
Sparse Core Ops, SparseCore 0:
  62.0 92.4 all-gather.2
